TPU v7x, 256 devices: a whole 4x4x8 slice. The times are simulated.
256 devices in a mesh: path: 16 (over z_hi, y, core), fsdp: 16 (over x, z_lo).
Axes of the slice: x: 4, y: 4, z: 8 (z_hi: 2, z_lo: 4; z = z_hi * 4 + z_lo), core: 2. Of those that a mesh axis runs over, the one named last changes fastest.
Arguments:
- inputs: bfloat16 [16, 2048, 2048], P('path', 'fsdp'), may hold values from -6 to 6
- targets: bfloat16 [16, 2048, 2048], P('path', 'fsdp'), may hold values from -6 to 6
- token_ids: int32 [16, 2048], P('path', 'fsdp'), may hold values from 0 to 31999, as said below
- module_table: int32 [16, 2], replicated, may hold values from 0 to 3, as said below
- path_weights: bfloat16 [16, 2, 2048, 5632], P('path', None, None, 'fsdp'), may hold values from -6 to 6
- master: float32 [2, 4, 2048, 5632], P(None, None, 'path', 'fsdp'), may hold values from -6 to 6
- momentum: float32 [2, 4, 2048, 5632], P(None, None, 'path', 'fsdp'), may hold values from -6 to 6
Outputs:
- new_weights: bfloat16 [16, 2, 2048, 5632], P('path', None, None, 'fsdp')
- new_master: float32 [2, 4, 2048, 5632], P(None, None, 'path', 'fsdp')
- new_momentum: float32 [2, 4, 2048, 5632], P(None, None, 'path', 'fsdp')
Inputs may be any that keep to these rules, and one draw needn't show every extreme that they name: `module_table`: at each level, every module is named by exactly 4 paths. `token_ids`: ids below 256 are control tokens.
All inputs are finite; a program needn't handle non-finite values.
Results may differ from a plain program's by a relative error of at most 0.014.
Values may be sent and summed in bfloat16 or wider, within the bound.
A program may use at most 128 MiB of HBM per device.

v0:
```python
import jax
import jax.numpy as jnp
from jax import lax
from jax.sharding import PartitionSpec as P

SPECIAL = 256


INNER_LR = 4096.0
OUTER_LR = 0.7
MOMENT = 0.9


def per_device(inputs, targets, token_ids, module_table, path_weights, master, momentum):
    x_local = inputs[0]
    w_in = path_weights[0, 0]
    w_out = path_weights[0, 1]
    width = w_in.shape[0]
    hidden_all = w_in.shape[1] * lax.axis_size("fsdp")
    out_scale = hidden_all ** (-0.5)
    x_full = lax.all_gather(x_local, "fsdp", axis=0, tiled=True)
    total = x_full.shape[0]
    pre = jnp.dot(x_full, w_in, preferred_element_type=jnp.float32) * width ** (-0.5)
    sig = jax.nn.sigmoid(pre)
    act = (pre * sig).astype(jnp.bfloat16)
    rows = act
    mine = lax.psum_scatter(
        (
            lax.dot_general(
                rows, w_out, (((1,), (1,)), ((), ())), preferred_element_type=jnp.float32
            )
            * out_scale
        ).astype(jnp.bfloat16),
        "fsdp",
        scatter_dimension=0,
        tiled=True,
    ).astype(jnp.float32)
    keep = (token_ids[0] >= SPECIAL).astype(jnp.float32)
    residual = x_local.astype(jnp.float32) + mine - targets[0].astype(jnp.float32)
    grad_mine = (keep[:, None] * residual / total).astype(jnp.bfloat16)
    piece = lax.all_gather(grad_mine, "fsdp", axis=0, tiled=True)
    rows = jnp.dot(piece, w_out, preferred_element_type=jnp.float32) * out_scale
    weight_acc = lax.dot_general(
        piece, act, (((0,), (0,)), ((), ())), preferred_element_type=jnp.float32
    )
    grad_out = weight_acc * out_scale
    pre_grad = (rows * sig * (1.0 + pre * (1.0 - sig))).astype(jnp.bfloat16)
    delta_out = INNER_LR * grad_out
    grad_in = lax.dot_general(
        x_full, pre_grad, (((0,), (0,)), ((), ())), preferred_element_type=jnp.float32
    ) * width ** (-0.5)
    stacked = jnp.stack([INNER_LR * grad_in, delta_out])[:, None]
    arrived = lax.all_to_all(
        stacked.astype(jnp.bfloat16), "path", split_axis=2, concat_axis=1, tiled=True
    ).astype(stacked.dtype)
    modules = master.shape[1]
    labels = jnp.arange(modules, dtype=jnp.int32)
    pick = (module_table.T[:, None, :] == labels[None, :, None]).astype(jnp.float32)
    counts = jnp.sum(pick, axis=2)
    sums = jnp.einsum("lmq,lqrc->lmrc", pick, arrived, precision=lax.Precision.HIGHEST)
    average = sums / counts[:, :, None, None]
    new_momentum = MOMENT * momentum + average
    new_master = master - OUTER_LR * (average + MOMENT * new_momentum)
    route = jnp.transpose(pick, (0, 2, 1)).astype(jnp.bfloat16)
    outgoing = jnp.einsum(
        "lqm,lmrc->lqrc", route, new_master.astype(jnp.bfloat16), preferred_element_type=jnp.float32
    ).astype(jnp.bfloat16)
    returned = lax.all_to_all(outgoing, "path", split_axis=1, concat_axis=2, tiled=True)
    new_weights = jnp.transpose(returned, (1, 0, 2, 3))
    return (new_weights, new_master, new_momentum)


def solution(mesh):
    in_specs = (
        P("path", "fsdp", None),
        P("path", "fsdp", None),
        P("path", "fsdp"),
        P(),
        P("path", None, None, "fsdp"),
        P(None, None, "path", "fsdp"),
        P(None, None, "path", "fsdp"),
    )
    out_specs = (
        P("path", None, None, "fsdp"),
        P(None, None, "path", "fsdp"),
        P(None, None, "path", "fsdp"),
    )
    return jax.shard_map(
        per_device, mesh=mesh, in_specs=in_specs, out_specs=out_specs, check_vma=False
    )
```

profile of v0, /device:TPU:121, one launch (start us, length us, event | category | flops | bytes accessed | tf_op | source)
XLA Modules:
  0.0 819.4 jit_solution(141483347020024842)
XLA Ops:
  7.2 0.0 all-gather.6.cloned.1.call-start
  7.2 0.7 all-gather.6.cloned.1.call-update
  7.9 0.0 reduce-scatter.2.cloned.1.call-start
  8.0 187.9 %all-gather.6.cloned.1.call-done = bf16[1,2048,2048]{2,1,0:T(8,128)(2,1)} async-done(((bf16[1,128,2048]{2,1,0:T(8,128)(2,1)}), bf16[1,2048,2048]{2,1,0:T(8,128)(2,1)}) %all-gather.6.cloned.1.call-update) | async-done | bytes 8388624 | tf_op jit(solution)/shard_map/all_gather | solution.py:21
  195.9 6.0 fusion.4
  201.9 1.6 copy-done.8
  203.5 7.0 multiply_convert_fusion
  210.5 0.0 reduce-scatter.2.cloned.1.call-update
  210.5 0.2 all-gather.4.cloned.1.call-start
  210.7 0.4 copy-done.7
  211.1 185.4 %reduce-scatter.2.cloned.1.call-done = bf16[128,2048]{1,0:T(8,128)(2,1)} async-done(((bf16[2048,2048]{1,0:T(8,128)(2,1)}), bf16[128,2048]{1,0:T(8,128)(2,1)}) %reduce-scatter.2.cloned.1.call-update) | async-done | bytes 524304 | tf_op jit(solution)/shard_map/reduce_scatter | solution.py:27
  396.5 2.1 fusion.30
  398.7 0.0 all-gather.4.cloned.1.call-update
  398.7 185.8 %all-gather.4.cloned.1.call-done = bf16[2048,2048]{1,0:T(8,128)(2,1)} async-done(((bf16[128,2048]{1,0:T(8,128)(2,1)}), bf16[2048,2048]{1,0:T(8,128)(2,1)}) %all-gather.4.cloned.1.call-update) | async-done | bytes 8388624 | tf_op jit(solution)/shard_map/all_gather | solution.py:41
  584.5 14.8 %fusion.17 = bf16[1,1,2048,352]{2,3,1,0:T(8,128)(2,1)} fusion(bf16[1,2048,2048]{2,1,0:T(8,128)(2,1)} %all-gather.6.cloned.1.call-done, f32[2048,352]{0,1:T(8,128)} %copy-done.8, bf16[2048,2048]{1,0:T(8,128)(2,1)} %all-gather.4.cloned.1.call-done, bf16[1,2,2048,352]{2,3,1,0:T(8,128)(2,1)} %param.11), kind=kOutput, calls=%fused_computation.17 | convolution fusion | flops 5914230784 | bytes 22544384 | tf_op jit(solution)/shard_map/dot_general | solution.py:49
  599.4 6.7 fusion.20
  606.0 0.3 pad_maximum_fusion
  606.3 5.9 copy.29
  612.2 10.4 %all-to-all-start = ((bf16[2,1,2048,352]{3,0,1,2:T(2,128)(2,1)}), bf16[2,1,2048,352]{3,0,1,2:T(2,128)(2,1)S(1)}, u32[]{:S(2)}, u32[]{:S(2)}) async-start(bf16[2,1,2048,352]{3,0,1,2:T(2,128)(2,1)} %copy.29), calls=%async_computation.1 | async-start | bytes 6291456 | tf_op jit(solution)/shard_map/all_to_all | solution.py:53
  622.6 0.1 convert_reduce_fusion
  622.7 118.7 %all-to-all-done = bf16[2,1,2048,352]{3,0,1,2:T(2,128)(2,1)S(1)} async-done(((bf16[2,1,2048,352]{3,0,1,2:T(2,128)(2,1)}), bf16[2,1,2048,352]{3,0,1,2:T(2,128)(2,1)S(1)}, u32[]{:S(2)}, u32[]{:S(2)}) %all-to-all-start) | async-done | bytes 2883616 | tf_op jit(solution)/shard_map/all_to_all | solution.py:53
  741.4 5.1 copy.39
  746.6 6.3 fusion.24
  752.9 1.1 copy-done
  754.0 1.3 convolution_convert_fusion
  755.3 2.3 copy.33
  757.6 4.5 all-to-all-start.1
  762.1 2.7 copy.35
  764.8 1.2 copy.36
  766.0 37.9 %all-to-all-done.1 = bf16[2,16,128,352]{2,3,0,1:T(8,128)(2,1)S(1)} async-done(((bf16[2,16,128,352]{2,3,0,1:T(8,128)(2,1)}), bf16[2,16,128,352]{2,3,0,1:T(8,128)(2,1)S(1)}, u32[]{:S(2)}, u32[]{:S(2)}) %all-to-all-start.1) | async-done | bytes 2883616 | tf_op jit(solution)/shard_map/all_to_all | solution.py:68
  803.9 3.4 copy.34
  807.3 5.5 transpose.18
  (18 shorter events, 0.0 us)
Async XLA Ops:
  7.2 188.7 %all-gather.6.cloned.1.call-start = ((), (), s32[]{:S(2)}) async-start(), calls=%async_computation.5 | async-start | bytes 8912896 | tf_op jit(solution)/shard_map/all_gather | solution.py:21
  7.9 195.6 %copy-start.6 = (bf16[1,2,2048,352]{2,3,1,0:T(8,128)(2,1)S(1)}, bf16[1,2,2048,352]{2,3,1,0:T(8,128)(2,1)}, u32[]{:S(2)}) copy-start(bf16[1,2,2048,352]{2,3,1,0:T(8,128)(2,1)} %param.11) | copy-start | bytes 8650756
  7.9 388.6 %reduce-scatter.2.cloned.1.call-start = ((), (), s32[]{:S(2)}) async-start(), calls=%async_computation.3 | async-start | bytes 8912896 | tf_op jit(solution)/shard_map/reduce_scatter | solution.py:27
  201.9 1.6 copy-start.8
  210.5 0.7 copy-start.7
  210.5 186.1 %copy-start.1 = (bf16[1,128,2048]{2,1,0:T(8,128)(2,1)S(1)}, bf16[1,128,2048]{2,1,0:T(8,128)(2,1)}, u32[]{:S(2)}) copy-start(bf16[1,128,2048]{2,1,0:T(8,128)(2,1)} %param.7) | copy-start | bytes 1572868
  210.5 186.1 %copy-start.4 = (bf16[1,128,2048]{2,1,0:T(8,128)(2,1)S(1)}, bf16[1,128,2048]{2,1,0:T(8,128)(2,1)}, u32[]{:S(2)}) copy-start(bf16[1,128,2048]{2,1,0:T(8,128)(2,1)} %param.8) | copy-start | bytes 1572868
  210.5 374.1 %all-gather.4.cloned.1.call-start = ((), (), s32[]{:S(2)}) async-start(), calls=%async_computation.4 | async-start | bytes 8912896 | tf_op jit(solution)/shard_map/all_gather | solution.py:41
  398.7 200.7 %copy-start.9 = (f32[2048,352]{0,1:T(8,128)S(1)}, f32[2048,352]{0,1:T(8,128)}, u32[]{:S(2)}) copy-start(f32[2048,352]{0,1:T(8,128)} %copy-done.8) | copy-start | bytes 8650756
  599.4 6.7 copy-start.3
  612.2 10.4 %copy-start.5 = (s32[16,2]{0,1:T(2,128)S(1)}, s32[16,2]{0,1:T(2,128)}, u32[]{:S(2)}) copy-start(s32[16,2]{0,1:T(2,128)} %param.10) | copy-start | bytes 388
  612.2 129.2 %all-to-all-start = ((bf16[2,1,2048,352]{3,0,1,2:T(2,128)(2,1)}), bf16[2,1,2048,352]{3,0,1,2:T(2,128)(2,1)S(1)}, u32[]{:S(2)}, u32[]{:S(2)}) async-start(bf16[2,1,2048,352]{3,0,1,2:T(2,128)(2,1)} %copy.29), calls=%async_computation.1 | async-start | bytes 6291456 | tf_op jit(solution)/shard_map/all_to_all | solution.py:53
  752.9 1.1 copy-start
  757.6 46.3 %all-to-all-start.1 = ((bf16[2,16,128,352]{2,3,0,1:T(8,128)(2,1)}), bf16[2,16,128,352]{2,3,0,1:T(8,128)(2,1)S(1)}, u32[]{:S(2)}, u32[]{:S(2)}) async-start(bf16[2,16,128,352]{2,3,0,1:T(8,128)(2,1)} %copy.33), calls=%async_computation.2 | async-start | bytes 5767168 | tf_op jit(solution)/shard_map/all_to_all | solution.py:68
  762.1 2.7 copy-start.2
Sparse Core Ops, SparseCore 0:
  9.8 186.0 all-gather.5
  210.6 185.8 reduce-scatter.1
  398.9 185.5 all-gather.3
where the time goes:
time: 820 us; the launch traced here: 819 us
  waiting for transfers between devices  717 us (87%)
  matrix products  42.1 us (5%)
  local copies, waits for them, and re-layouts  29.3 us (4%)
  starting transfers between devices  15.2 us (2%)
  between operations  13.8 us (2%)
    all_gather x1, waiting for transfers between devices, per_device(): x_full = lax.all_gather(x_local, 'fsdp', axis=0, tiled=True)  188 us
    all_gather x1, waiting for transfers between devices, per_device(): piece = lax.all_gather(grad_mine, 'fsdp', axis=0, tiled=True)  186 us
    reduce_scatter x1, waiting for transfers between devices, per_device(): lax.psum_scatter((lax.dot_general(rows, w_out, (((1,), (1,)), ((), ())),...  185 us
    all_to_all x1, waiting for transfers between devices, per_device(): lax.all_to_all(stacked.astype(jnp.bfloat16), 'path', split_axis=2, concat...  119 us
    all_to_all x1, waiting for transfers between devices, per_device(): lax.all_to_all(outgoing, 'path', split_axis=1, concat_axis=2, tiled=True)  37.9 us
  transfers between devices with their start and end apart: 5, of which 5 were waited for; matrix products, arithmetic and copies ran while one was open for 0% of the time, Pallas kernels for 0%

commit v1 on v0

v1 whole, which is shorter than its diff:
```python
import functools

import jax
import jax.numpy as jnp
from jax import lax
from jax.experimental import pallas as pl
from jax.experimental.pallas import tpu as pltpu
from jax.sharding import PartitionSpec as P

SPECIAL = 256
INNER_LR = 4096.0
OUTER_LR = 0.7
MOMENT = 0.9
MESH = pl.DeviceIdType.MESH

RA, RB = 96, 32
HA, HB = RA // 2, RB // 2
NX, NZ = 4, 4
ROWS_A = NX * NZ * RA
SUPER = NX * RB


class Place:
    def __init__(self):
        f = lax.axis_index("fsdp")
        self.x, self.z = f // NZ, f % NZ
        self.far = self.z // 2
        self.w = (self.z + self.far) % 2
        flip = 1 - 2 * self.far
        self.flip = flip
        self.right = ((self.x + 1) % NX) * NZ + self.z
        self.left = ((self.x + NX - 1) % NX) * NZ + self.z
        self.inner = self.x * NZ + self.z + flip
        self.edge = self.x * NZ + self.z - flip

    def zb(self, r):
        swap = jnp.where(r == 0, 1, jnp.where(r == 1, -1, 0))
        o = r + self.w * swap
        return o * self.flip + (NZ - 1) * self.far

    def col(self, dx):
        return (self.x + dx + NX) % NX


def rows_a(x, z):
    return pl.multiple_of((x * NZ + z) * RA, 16)


def rows_b(x, z):
    return pl.multiple_of(ROWS_A + (z * NX + x) * RB, 16)


def rows_super(z):
    return pl.multiple_of(ROWS_A + z * SUPER, 16)


def rcopy(src, dst, ssem, rsem, f):
    return pltpu.make_async_remote_copy(
        src_ref=src, dst_ref=dst, send_sem=ssem, recv_sem=rsem, device_id={"fsdp": f}, device_id_type=MESH
    )


def gather(pp, buf, ssem, rsem, compute):
    x, z, w = pp.x, pp.z, pp.w

    def piece(start, n):
        return buf.at[pl.ds(start, n)]

    def push(kind, side, i, start, n, f, slot):
        rcopy(piece(start, n), piece(start, n), ssem.at[kind, side, i], rsem.at[kind, slot[0], slot[1]], f).start()

    def arrived(kind, side, i, start, n):
        rcopy(piece(start, n), piece(start, n), ssem.at[kind, side, i], rsem.at[kind, side, i], pp.right).wait_recv()

    def sent(kind, side, i, n):
        rcopy(piece(0, n), piece(0, n), ssem.at[kind, side, i], rsem.at[kind, side, i], pp.right).wait_send()

    own_a, own_b = rows_a(x, z), rows_b(x, z)

    def z_own(kind, start, n):
        push(kind, 0, 0, start, n, pp.inner, (0, z))

        @pl.when(w == 1)
        def _():
            push(kind, 1, 0, start, n, pp.edge, (0, z))

    def z_forward(kind, r, zb, start, n):
        @pl.when((w == 1) & (r == 1))
        def _():
            push(kind, 0, r, start, n, pp.inner, (0, zb))

        @pl.when((w == 1) & (r >= 2))
        def _():
            push(kind, 1, r, start, n, pp.edge, (0, zb))

    z_own(0, own_a, RA)
    for side, f in ((0, pp.right), (1, pp.left)):
        push(3, side, 0, own_b, RB, f, (side, 0))

    def step(t, carry):
        zt = pp.zb(t)
        col_t = rows_a(x, zt)

        @pl.when((t >= 1) & (t <= 3))
        def _():
            arrived(0, 0, zt, col_t, RA)
            z_forward(0, t, zt, col_t, RA)

        @pl.when(t <= 3)
        def _():
            for side, f in ((0, pp.right), (1, pp.left)):
                push(1, side, t, col_t, RA, f, (side, t))

        @pl.when(t == 0)
        def _():
            for side, dx, f in ((0, -1, pp.right), (1, 1, pp.left)):
                start = rows_b(pp.col(dx), z)
                arrived(3, side, 0, start, RB)
                push(4, side, 0, pl.multiple_of(start + side * HB, 16), HB, f, (side, 0))

        zl = pp.zb(t - 1)

        @pl.when((t >= 1) & (t <= 4))
        def _():
            for side, dx, f in ((0, -1, pp.right), (1, 1, pp.left)):
                start = rows_a(pp.col(dx), zl)
                arrived(1, side, t - 1, start, RA)
                push(2, side, t - 1, pl.multiple_of(start + side * HA, 16), HA, f, (side, t - 1))

        @pl.when(t == 1)
        def _():
            start = rows_b(pp.col(2), z)
            for side in (0, 1):
                arrived(4, side, 0, pl.multiple_of(start + side * HB, 16), HB)
            z_own(5, rows_super(z), SUPER)

        @pl.when((t >= 2) & (t <= 4))
        def _():
            arrived(5, 0, zl, rows_super(zl), SUPER)
            z_forward(5, t - 1, zl, rows_super(zl), SUPER)

        @pl.when(t <= 3)
        def _():
            compute(col_t, RA)

        @pl.when((t >= 1) & (t <= 4))
        def _():
            def sides(j, c):
                compute(rows_a(pp.col(2 * j - 1), zl), RA)
                return c

            lax.fori_loop(0, 2, sides, 0)
            compute(rows_super(zl), SUPER)

        @pl.when(t >= 2)
        def _():
            start = rows_a(pp.col(2), pp.zb(t - 2))
            for side in (0, 1):
                arrived(2, side, t - 2, pl.multiple_of(start + side * HA, 16), HA)
            compute(start, RA)

        return carry

    lax.fori_loop(0, 6, step, 0)

    for kind, n in ((0, RA), (5, SUPER)):
        sent(kind, 0, 0, n)

        @pl.when(w == 1)
        def _():
            sent(kind, 1, 0, n)
            sent(kind, 0, 1, n)
            sent(kind, 1, 2, n)
            sent(kind, 1, 3, n)

    for side in (0, 1):
        sent(3, side, 0, RB)
        sent(4, side, 0, HB)

        def drain(i, c):
            sent(1, side, i, RA)
            sent(2, side, i, HA)
            return c

        lax.fori_loop(0, 4, drain, 0)


COLS = 512


def reduce(pp, partial, sc):
    x, z, w = pp.x, pp.z, pp.w
    width = sc.acc_a.shape[1]
    ssem, rsem = sc.rs_send, sc.rs_recv

    def chunks(body):
        def run(k, c):
            body(pl.ds(pl.multiple_of(k * COLS, 128), COLS))
            return c

        lax.fori_loop(0, width // COLS, run, 0)

    def push(src, dst, kind, side, i, f, slot):
        rcopy(src, dst, ssem.at[kind, side, i], rsem.at[kind, slot[0], slot[1]], f).start()

    def arrived(ref, kind, side, i):
        rcopy(ref, ref, ssem.at[kind, side, i], rsem.at[kind, side, i], pp.right).wait_recv()

    def sent(ref, kind, side, i):
        rcopy(ref, ref, ssem.at[kind, side, i], rsem.at[kind, side, i], pp.right).wait_send()

    def up(v):
        return v.astype(jnp.float32)

    def z_stage(kind, r, acc, recv, send):
        @pl.when((w == 1) & (r >= 1))
        def _():
            arrived(recv.at[r], kind, 0, r)

            def add(cs):
                send[r, :, cs] = (acc[:, cs] + up(recv[r, :, cs])).astype(jnp.bfloat16)

            chunks(add)

        @pl.when((w == 1) & (r >= 2))
        def _():
            slot = jnp.where(r == 3, 1, 0)
            push(send.at[r], recv.at[slot], kind, 0, r, pp.inner, (0, slot))

        @pl.when((w == 1) & (r == 1))
        def _():
            push(send.at[r], recv.at[0], kind, 0, r, pp.edge, (0, 0))

        @pl.when((w == 0) & (r >= 1))
        def _():
            def cast(cs):
                send[r, :, cs] = acc[:, cs].astype(jnp.bfloat16)

            chunks(cast)
            slot = jnp.where(r == 1, 4, r)
            push(send.at[r], recv.at[slot], kind, 0, r, pp.inner, (0, slot))

        @pl.when(r == 0)
        def _():
            arrived(recv.at[0], kind, 0, 0)

            def add(cs):
                acc[:, cs] = acc[:, cs] + up(recv[0, :, cs])

            chunks(add)

        @pl.when((w == 1) & (r == 0))
        def _():
            arrived(recv.at[4], kind, 0, 4)

            def add(cs):
                acc[:, cs] = acc[:, cs] + up(recv[4, :, cs])

            chunks(add)

    def b_round(r):
        start = rows_super(pp.zb(r))

        def fill(cs):
            sc.acc_b[:, cs] = partial(start, SUPER, cs)

        chunks(fill)
        z_stage(4, r, sc.acc_b, sc.b_recv, sc.b_send)

    def step(t, carry):
        r0, r1, r2 = 3 - t, 4 - t, 5 - t

        @pl.when(t <= 3)
        def _():
            start = rows_a(pp.col(2), pp.zb(r0))

            def fill(cs):
                sc.h_send[r0, :, cs] = partial(start, RA, cs).astype(jnp.bfloat16)

            chunks(fill)
            push(sc.h_send.at[r0, pl.ds(0, HA)], sc.h_recv.at[1, r0], 0, 1, r0, pp.left, (1, r0))
            push(sc.h_send.at[r0, pl.ds(HA, HA)], sc.h_recv.at[0, r0], 0, 0, r0, pp.right, (0, r0))

        @pl.when((t == 0) & (w == 0))
        def _():
            def run(i, c):
                b_round(3 - i)
                return c

            lax.fori_loop(0, 3, run, 0)

        @pl.when((t >= 1) & (t <= 4))
        def _():
            zr = pp.zb(r1)
            for side, dx, f, lo in ((0, 1, pp.right, HA), (1, -1, pp.left, 0)):
                start = rows_a(pp.col(dx), zr)
                arrived(sc.h_recv.at[side, r1], 0, side, r1)

                def fill(cs):
                    part = partial(start, RA, cs)
                    got = up(sc.h_recv[side, r1, :, cs])
                    both = part[lo : lo + HA] + got
                    alone = part[HA - lo : HA - lo + HA]
                    sc.f_send[side, r1, pl.ds(lo, HA), cs] = both.astype(jnp.bfloat16)
                    sc.f_send[side, r1, pl.ds(HA - lo, HA), cs] = alone.astype(jnp.bfloat16)

                chunks(fill)
                push(sc.f_send.at[side, r1], sc.f_recv.at[side, r1], 1, side, r1, f, (side, r1))

        @pl.when((t >= 1) & (t <= 3) & (w == 1))
        def _():
            b_round(r1)

        @pl.when(t == 4)
        def _():
            b_round(0)
            start = pl.multiple_of(pp.col(2) * RB, RB)
            sc.bh_send[...] = sc.acc_b[pl.ds(start, RB), :].astype(jnp.bfloat16)
            push(sc.bh_send.at[pl.ds(0, HB)], sc.bh_recv.at[1], 2, 1, 0, pp.left, (1, 0))
            push(sc.bh_send.at[pl.ds(HB, HB)], sc.bh_recv.at[0], 2, 0, 0, pp.right, (0, 0))

        @pl.when(t >= 2)
        def _():
            start = rows_a(x, pp.zb(r2))
            for side in (0, 1):
                arrived(sc.f_recv.at[side, r2], 1, side, r2)

            def fill(cs):
                sc.acc_a[:, cs] = partial(start, RA, cs) + up(sc.f_recv[0, r2, :, cs]) + up(sc.f_recv[1, r2, :, cs])

            chunks(fill)
            z_stage(3, r2, sc.acc_a, sc.a_recv, sc.a_send)

        @pl.when(t == 4)
        def _():
            for side, dx, f, lo in ((0, 1, pp.right, HB), (1, -1, pp.left, 0)):
                start = pl.multiple_of(pp.col(dx) * RB, RB)
                arrived(sc.bh_recv.at[side], 2, side, 0)

                def fill(cs):
                    got = up(sc.bh_recv[side, :, cs])
                    both = sc.acc_b[pl.ds(pl.multiple_of(start + lo, 8), HB), cs] + got
                    alone = sc.acc_b[pl.ds(pl.multiple_of(start + HB - lo, 8), HB), cs]
                    sc.bf_send[side, pl.ds(lo, HB), cs] = both.astype(jnp.bfloat16)
                    sc.bf_send[side, pl.ds(HB - lo, HB), cs] = alone.astype(jnp.bfloat16)

                chunks(fill)
                push(sc.bf_send.at[side], sc.bf_recv.at[side], 5, side, 0, f, (side, 0))

        return carry

    lax.fori_loop(0, 6, step, 0)
    for side in (0, 1):
        arrived(sc.bf_recv.at[side], 5, side, 0)
    own = pl.multiple_of(x * RB, RB)

    def last(cs):
        sc.fin_b[:, cs] = sc.acc_b[pl.ds(own, RB), cs] + up(sc.bf_recv[0, :, cs]) + up(sc.bf_recv[1, :, cs])

    chunks(last)

    for side in (0, 1):
        sent(sc.bh_recv.at[side], 2, side, 0)
        sent(sc.bf_send.at[side], 5, side, 0)

        def drain(i, c):
            sent(sc.h_recv.at[side, i], 0, side, i)
            sent(sc.f_send.at[side, i], 1, side, i)
            return c

        lax.fori_loop(0, 4, drain, 0)

    def drain_z(i, c):
        sent(sc.a_send.at[i], 3, 0, i)
        sent(sc.b_send.at[i], 4, 0, i)
        return c

    lax.fori_loop(1, 4, drain_z, 0)


class Refs:
    def __init__(self, **kw):
        self.__dict__.update(kw)


def scratch(width, hidden):
    bf, f32 = jnp.bfloat16, jnp.float32
    tokens = NX * NZ * (RA + RB)
    v = pltpu.VMEM
    return dict(
        xg=v((tokens, width), bf),
        og=v((tokens, width), bf),
        w_in=v((width, hidden), bf),
        w_out=v((width, hidden), bf),
        w_out_t=v((hidden, width), bf),
        act=v((tokens, hidden), bf),
        slope=v((tokens, hidden), f32),
        pre_grad=v((tokens, hidden), bf),
        tgt=v((RA + RB, width), bf),
        h_send=v((4, RA, width), bf),
        h_recv=v((2, 4, HA, width), bf),
        f_send=v((2, 4, RA, width), bf),
        f_recv=v((2, 4, RA, width), bf),
        a_send=v((4, RA, width), bf),
        a_recv=v((5, RA, width), bf),
        b_send=v((4, SUPER, width), bf),
        b_recv=v((5, SUPER, width), bf),
        bh_send=v((RB, width), bf),
        bh_recv=v((2, HB, width), bf),
        bf_send=v((2, RB, width), bf),
        bf_recv=v((2, RB, width), bf),
        acc_a=v((RA, width), f32),
        acc_b=v((SUPER, width), f32),
        fin_b=v((RB, width), f32),
        g1_send=pltpu.SemaphoreType.DMA((6, 2, 4)),
        g1_recv=pltpu.SemaphoreType.DMA((6, 2, 4)),
        g2_send=pltpu.SemaphoreType.DMA((6, 2, 4)),
        g2_recv=pltpu.SemaphoreType.DMA((6, 2, 4)),
        rs_send=pltpu.SemaphoreType.DMA((6, 2, 5)),
        rs_recv=pltpu.SemaphoreType.DMA((6, 2, 5)),
        local=pltpu.SemaphoreType.DMA((5,)),
    )


def step_kernel(names, width_scale, hidden_scale, tokens, x_ref, t_ref, keep_ref, w_ref, delta_ref, *refs):
    sc = Refs(**dict(zip(names, refs)))
    pp = Place()
    x, z, w = pp.x, pp.z, pp.w
    own_a, own_b = rows_a(x, z), rows_b(x, z)

    loads = [
        pltpu.make_async_copy(x_ref.at[pl.ds(0, RA)], sc.xg.at[pl.ds(own_a, RA)], sc.local.at[0]),
        pltpu.make_async_copy(x_ref.at[pl.ds(RA, RB)], sc.xg.at[pl.ds(own_b, RB)], sc.local.at[1]),
        pltpu.make_async_copy(w_ref.at[0], sc.w_in, sc.local.at[2]),
        pltpu.make_async_copy(w_ref.at[1], sc.w_out, sc.local.at[3]),
        pltpu.make_async_copy(t_ref, sc.tgt, sc.local.at[4]),
    ]
    for c in loads:
        c.start()

    barrier = pltpu.get_barrier_semaphore()
    for f in (pp.right, pp.left, pp.inner):
        pl.semaphore_signal(barrier, inc=1, device_id={"fsdp": f}, device_id_type=MESH)

    @pl.when(w == 1)
    def _():
        pl.semaphore_signal(barrier, inc=1, device_id={"fsdp": pp.edge}, device_id_type=MESH)

    pl.semaphore_wait(barrier, 3 + w)
    for c in loads:
        c.wait()

    def forward(start, n):
        rows = pl.ds(start, n)
        pre = jnp.dot(sc.xg[rows, :], sc.w_in[...], preferred_element_type=jnp.float32) * width_scale
        sig = jax.nn.sigmoid(pre)
        sc.act[rows, :] = (pre * sig).astype(jnp.bfloat16)
        sc.slope[rows, :] = sig * (1.0 + pre * (1.0 - sig))

    gather(pp, sc.xg, sc.g1_send, sc.g1_recv, forward)

    for k in range(0, sc.w_out.shape[0], 256):
        sc.w_out_t[:, k : k + 256] = sc.w_out[k : k + 256, :].T

    def partial(start, n, cs):
        return jnp.dot(sc.act[pl.ds(start, n), :], sc.w_out_t[:, cs], preferred_element_type=jnp.float32) * hidden_scale

    reduce(pp, partial, sc)

    def loss_grad(total, own, lo, n):
        res = sc.xg[pl.ds(own, n), :].astype(jnp.float32) + total[...] - sc.tgt[pl.ds(lo, n), :].astype(jnp.float32)
        sc.og[pl.ds(own, n), :] = (keep_ref[pl.ds(lo, n), :] * res / tokens).astype(jnp.bfloat16)

    loss_grad(sc.acc_a, own_a, 0, RA)
    loss_grad(sc.fin_b, own_b, RA, RB)

    def backward(start, n):
        rows = pl.ds(start, n)
        act_grad = jnp.dot(sc.og[rows, :], sc.w_out[...], preferred_element_type=jnp.float32) * hidden_scale
        sc.pre_grad[rows, :] = (act_grad * sc.slope[rows, :]).astype(jnp.bfloat16)

    gather(pp, sc.og, sc.g2_send, sc.g2_recv, backward)

    def grads(level, left, right, scale):
        def run(k, c):
            cols = pl.ds(pl.multiple_of(k * 256, 256), 256)
            g = lax.dot_general(
                left[:, cols], right[...], (((0,), (0,)), ((), ())), preferred_element_type=jnp.float32
            )
            delta_ref[level, cols, :] = (INNER_LR * scale * g).astype(jnp.bfloat16)
            return c

        lax.fori_loop(0, left.shape[1] // 256, run, 0)

    grads(1, sc.og, sc.act, hidden_scale)
    grads(0, sc.xg, sc.pre_grad, width_scale)


def per_device(inputs, targets, token_ids, module_table, path_weights, master, momentum):
    width, hidden = path_weights.shape[2:]
    n = lax.axis_size("fsdp")
    tokens = inputs.shape[1] * n
    keep = (token_ids[0] >= SPECIAL).astype(jnp.float32)[:, None]
    spec = scratch(width, hidden)
    hbm = pl.BlockSpec(memory_space=pl.ANY)
    vmem = pl.BlockSpec(memory_space=pltpu.VMEM)
    delta = pl.pallas_call(
        functools.partial(step_kernel, tuple(spec), width ** (-0.5), (hidden * n) ** (-0.5), tokens),
        out_shape=jax.ShapeDtypeStruct((2, width, hidden), jnp.bfloat16),
        in_specs=[hbm, hbm, vmem, hbm],
        out_specs=vmem,
        scratch_shapes=list(spec.values()),
        compiler_params=pltpu.CompilerParams(
            collective_id=0, has_side_effects=True, vmem_limit_bytes=62 * 1024 * 1024
        ),
        name="inner_step",
    )(inputs[0], targets[0], keep, path_weights[0])

    arrived = lax.all_to_all(delta[:, None], "path", split_axis=2, concat_axis=1, tiled=True).astype(jnp.float32)
    modules = master.shape[1]
    labels = jnp.arange(modules, dtype=jnp.int32)
    pick = (module_table.T[:, None, :] == labels[None, :, None]).astype(jnp.float32)
    counts = jnp.sum(pick, axis=2)
    sums = jnp.einsum("lmq,lqrc->lmrc", pick, arrived, precision=lax.Precision.HIGHEST)
    average = sums / counts[:, :, None, None]
    new_momentum = MOMENT * momentum + average
    new_master = master - OUTER_LR * (average + MOMENT * new_momentum)
    route = jnp.transpose(pick, (0, 2, 1)).astype(jnp.bfloat16)
    outgoing = jnp.einsum(
        "lqm,lmrc->lqrc", route, new_master.astype(jnp.bfloat16), preferred_element_type=jnp.float32
    ).astype(jnp.bfloat16)
    returned = lax.all_to_all(outgoing, "path", split_axis=1, concat_axis=2, tiled=True)
    new_weights = jnp.transpose(returned, (1, 0, 2, 3))
    return (new_weights, new_master, new_momentum)


def solution(mesh):
    in_specs = (
        P("path", "fsdp", None),
        P("path", "fsdp", None),
        P("path", "fsdp"),
        P(),
        P("path", None, None, "fsdp"),
        P(None, None, "path", "fsdp"),
        P(None, None, "path", "fsdp"),
    )
    out_specs = (
        P("path", None, None, "fsdp"),
        P(None, None, "path", "fsdp"),
        P(None, None, "path", "fsdp"),
    )
    return jax.shard_map(
        per_device, mesh=mesh, in_specs=in_specs, out_specs=out_specs, check_vma=False
    )
```

time: 820 us -> 410 us (0.50)
  waiting for transfers between devices: 717 us -> 120 us
  Pallas kernels: 0 us -> 218 us
  matrix products: 42.1 us -> 7.59 us
  between operations: 13.8 us -> 0.67 us
    all_gather x2 -> x0, waiting for transfers between devices: 374 us -> none  [the longest x1 188 us: per_device(): x_full = lax.all_gather(x_local, 'fsdp', axis=0, tiled=True)]
    pallas_call x0 -> x1, Pallas kernels: none -> 218 us  [per_device(): pl.pallas_call(functools.partial(step_kernel, tuple(spec), width ** (-0.5...]
    reduce_scatter x1 -> x0, waiting for transfers between devices: 185 us -> none  [per_device(): lax.psum_scatter((lax.dot_general(rows, w_out, (((1,), (1,)), ((), ())),...]
    all_to_all x1, waiting for transfers between devices: 119 us -> 79.6 us  [per_device(): lax.all_to_all(delta[:, None], 'path', split_axis=2, concat_axis=1, tiled...]
    dot_general x4 -> x0, matrix products: 34.5 us -> none  [the longest x1 14.8 us: per_device(): lax.dot_general(x_full, pre_grad, (((0,), (0,)), ((), ())), preferred_ele...]
  transfers between devices with their start and end apart: 5 -> 2, of which waited for: 5 -> 2; matrix products, arithmetic and copies ran while one was open for 0% -> 1% of each run, Pallas kernels for 0% -> 0%
where the time goes in v1:
time: 410 us; the launch traced here: 404 us
  Pallas kernels  218 us (53%)
  waiting for transfers between devices  120 us (29%)
  local copies, waits for them, and re-layouts  34.8 us (8%)
  starting transfers between devices  21.5 us (5%)
  matrix products  7.59 us (2%)
    pallas_call x1, Pallas kernels, per_device(): pl.pallas_call(functools.partial(step_kernel, tuple(spec), width ** (-0.5...  218 us
    all_to_all x1, waiting for transfers between devices, per_device(): lax.all_to_all(delta[:, None], 'path', split_axis=2, concat_axis=1, tiled...  79.6 us
    all_to_all x1, waiting for transfers between devices, per_device(): lax.all_to_all(outgoing, 'path', split_axis=1, concat_axis=2, tiled=True)  40.8 us
    all_to_all x1, starting transfers between devices, per_device(): lax.all_to_all(delta[:, None], 'path', split_axis=2, concat_axis=1, tiled...  16.9 us
    unnamed x9, local copies, waits for them, and re-layouts  9.6 us
  transfers between devices with their start and end apart: 2, of which 2 were waited for; matrix products, arithmetic and copies ran while one was open for 1% of the time, Pallas kernels for 0%

profile of v1, /device:TPU:121, one launch (start us, length us, event | category | flops | bytes accessed | tf_op | source)
XLA Modules:
  0.0 403.8 jit_solution(8263573670975524606)
XLA Ops:
  0.6 0.7 fusion.8
  1.3 0.7 copy.27.keep_ref
  2.0 4.6 %copy.26 = bf16[1,2,2048,352]{3,2,1,0:T(8,128)(2,1)} copy(bf16[1,2,2048,352]{2,3,1,0:T(8,128)(2,1)} %param.11) | data formatting | bytes 5767168 | tf_op args[4]
  6.6 218.1 %inner_step.1 = bf16[2,2048,352]{2,1,0:T(8,128)(2,1)} custom-call(bf16[128,2048]{1,0:T(8,128)(2,1)} %bitcast.28, bf16[128,2048]{1,0:T(8,128)(2,1)} %bitcast.29, f32[128,1]{1,0:T(8,128)} %copy.27.keep_ref, bf16[2,2048,352]{2,1,0:T(8,128)(2,1)} %bitcast.26), custom_call_target="tpu_custom_call" | custom-call | tf_op jit(solution)/shard_map/inner_step/pallas_call | solution.py:507
  224.7 8.0 %copy.28 = bf16[2,1,2048,352]{3,0,1,2:T(2,128)(2,1)} copy(bf16[2,1,2048,352]{3,2,0,1:T(8,128)(2,1)} %bitcast.25) | data formatting | bytes 5767168 | tf_op jit(solution)/shard_map/broadcast_in_dim | solution.py:519
  232.7 0.0 copy-start.2
  232.7 16.9 %all-to-all-start = ((bf16[2,1,2048,352]{3,0,1,2:T(2,128)(2,1)}), bf16[2,1,2048,352]{3,0,1,2:T(2,128)(2,1)S(1)}, u32[]{:S(2)}, u32[]{:S(2)}) async-start(bf16[2,1,2048,352]{3,0,1,2:T(2,128)(2,1)} %copy.28), calls=%async_computation | async-start | bytes 6291456 | tf_op jit(solution)/shard_map/all_to_all | solution.py:519
  249.6 0.0 copy-done.2
  249.6 0.1 convert_reduce_fusion
  249.7 79.6 %all-to-all-done = bf16[2,1,2048,352]{3,0,1,2:T(2,128)(2,1)S(1)} async-done(((bf16[2,1,2048,352]{3,0,1,2:T(2,128)(2,1)}), bf16[2,1,2048,352]{3,0,1,2:T(2,128)(2,1)S(1)}, u32[]{:S(2)}, u32[]{:S(2)}) %all-to-all-start) | async-done | bytes 2883616 | tf_op jit(solution)/shard_map/all_to_all | solution.py:519
  329.3 5.1 %copy.38 = bf16[2,16,128,352]{2,1,3,0:T(8,128)(2,1)} copy(bf16[2,16,128,352]{3,0,2,1:T(2,128)(2,1)S(1)} %bitcast.27) | data formatting | bytes 5767168 | tf_op jit(solution)/shard_map/all_to_all | solution.py:519
  334.5 6.3 %fusion = (f32[2,4,128,352]{2,1,3,0:T(4,128)}, f32[2,4,128,352]{2,1,3,0:T(4,128)S(1)}) fusion(f32[2,4,128,352]{2,3,1,0:T(8,128)} %param.13, f32[2,4,128,352]{2,3,1,0:T(8,128)} %param.12, f32[2,4]{1,0:T(2,128)S(1)} %convert_reduce_fusion, bf16[2,16,128,352]{2,1,3,0:T(8,128)(2,1)} %copy.38, s32[2,16]{1,0:T(2,128)S(1)} %bitcast.31), kind=kOutput, calls=%fused_computation.4 | convolution fusion | flops 14057600 | bytes 8650912 | tf_op jit(solution)/shard_map/lmq,lqrc->lmrc/dot_general | solution.py:524
  340.8 0.0 copy-start
  340.8 1.1 copy-done
  341.9 1.3 convolution_convert_fusion
  343.2 2.3 copy.32
  345.5 4.6 %all-to-all-start.1 = ((bf16[2,16,128,352]{2,3,0,1:T(8,128)(2,1)}), bf16[2,16,128,352]{2,3,0,1:T(8,128)(2,1)S(1)}, u32[]{:S(2)}, u32[]{:S(2)}) async-start(bf16[2,16,128,352]{2,3,0,1:T(8,128)(2,1)} %copy.32), calls=%async_computation.1 | async-start | bytes 5767168 | tf_op jit(solution)/shard_map/all_to_all | solution.py:532
  350.1 0.0 copy-start.1
  350.1 2.7 copy.34
  352.8 0.0 copy-done.1
  352.8 1.2 copy.35
  354.0 40.8 %all-to-all-done.1 = bf16[2,16,128,352]{2,3,0,1:T(8,128)(2,1)S(1)} async-done(((bf16[2,16,128,352]{2,3,0,1:T(8,128)(2,1)}), bf16[2,16,128,352]{2,3,0,1:T(8,128)(2,1)S(1)}, u32[]{:S(2)}, u32[]{:S(2)}) %all-to-all-start.1) | async-done | bytes 2883616 | tf_op jit(solution)/shard_map/all_to_all | solution.py:532
  394.8 3.4 copy.33
  398.2 5.5 %transpose.11 = bf16[1,2,2048,352]{2,3,1,0:T(8,128)(2,1)} reshape(bf16[2,16,128,352]{2,1,3,0:T(8,128)(2,1)} %copy.33) | data formatting | bytes 5767168 | tf_op jit(solution)/shard_map/transpose | solution.py:533
Async XLA Ops:
  232.7 16.9 %copy-start.2 = (s32[16,2]{0,1:T(2,128)S(1)}, s32[16,2]{0,1:T(2,128)}, u32[]{:S(2)}) copy-start(s32[16,2]{0,1:T(2,128)} %param.10) | copy-start | bytes 388
  232.7 96.7 %all-to-all-start = ((bf16[2,1,2048,352]{3,0,1,2:T(2,128)(2,1)}), bf16[2,1,2048,352]{3,0,1,2:T(2,128)(2,1)S(1)}, u32[]{:S(2)}, u32[]{:S(2)}) async-start(bf16[2,1,2048,352]{3,0,1,2:T(2,128)(2,1)} %copy.28), calls=%async_computation | async-start | bytes 6291456 | tf_op jit(solution)/shard_map/all_to_all | solution.py:519
  340.8 1.1 copy-start
  345.5 49.3 %all-to-all-start.1 = ((bf16[2,16,128,352]{2,3,0,1:T(8,128)(2,1)}), bf16[2,16,128,352]{2,3,0,1:T(8,128)(2,1)S(1)}, u32[]{:S(2)}, u32[]{:S(2)}) async-start(bf16[2,16,128,352]{2,3,0,1:T(8,128)(2,1)} %copy.32), calls=%async_computation.1 | async-start | bytes 5767168 | tf_op jit(solution)/shard_map/all_to_all | solution.py:532
  350.1 2.7 copy-start.1

commit v2 on v1

--- a/solution.py
+++ b/solution.py
@@ -218,27 +218,27 @@
             arrived(recv.at[r], kind, 0, r)
 
             def add(cs):
-                send[r, :, cs] = (acc[:, cs] + up(recv[r, :, cs])).astype(jnp.bfloat16)
+                send[r - 1, :, cs] = (acc[:, cs] + up(recv[r, :, cs])).astype(jnp.bfloat16)
 
             chunks(add)
 
         @pl.when((w == 1) & (r >= 2))
         def _():
             slot = jnp.where(r == 3, 1, 0)
-            push(send.at[r], recv.at[slot], kind, 0, r, pp.inner, (0, slot))
+            push(send.at[r - 1], recv.at[slot], kind, 0, r, pp.inner, (0, slot))
 
         @pl.when((w == 1) & (r == 1))
         def _():
-            push(send.at[r], recv.at[0], kind, 0, r, pp.edge, (0, 0))
+            push(send.at[r - 1], recv.at[0], kind, 0, r, pp.edge, (0, 0))
 
         @pl.when((w == 0) & (r >= 1))
         def _():
             def cast(cs):
-                send[r, :, cs] = acc[:, cs].astype(jnp.bfloat16)
+                send[r - 1, :, cs] = acc[:, cs].astype(jnp.bfloat16)
 
             chunks(cast)
             slot = jnp.where(r == 1, 4, r)
-            push(send.at[r], recv.at[slot], kind, 0, r, pp.inner, (0, slot))
+            push(send.at[r - 1], recv.at[slot], kind, 0, r, pp.inner, (0, slot))
 
         @pl.when(r == 0)
         def _():
@@ -371,8 +371,8 @@
         lax.fori_loop(0, 4, drain, 0)
 
     def drain_z(i, c):
-        sent(sc.a_send.at[i], 3, 0, i)
-        sent(sc.b_send.at[i], 4, 0, i)
+        sent(sc.a_send.at[i - 1], 3, 0, i)
+        sent(sc.b_send.at[i - 1], 4, 0, i)
         return c
 
     lax.fori_loop(1, 4, drain_z, 0)
@@ -383,16 +383,15 @@
         self.__dict__.update(kw)
 
 
-def scratch(width, hidden):
+def scratch(width, hidden, modules, rows):
     bf, f32 = jnp.bfloat16, jnp.float32
     tokens = NX * NZ * (RA + RB)
     v = pltpu.VMEM
     return dict(
         xg=v((tokens, width), bf),
         og=v((tokens, width), bf),
-        w_in=v((width, hidden), bf),
-        w_out=v((width, hidden), bf),
-        w_out_t=v((hidden, width), bf),
+        w_in=v((hidden, width), bf),
+        w_out=v((hidden, width), bf),
         act=v((tokens, hidden), bf),
         slope=v((tokens, hidden), f32),
         pre_grad=v((tokens, hidden), bf),
@@ -401,9 +400,9 @@
         h_recv=v((2, 4, HA, width), bf),
         f_send=v((2, 4, RA, width), bf),
         f_recv=v((2, 4, RA, width), bf),
-        a_send=v((4, RA, width), bf),
+        a_send=v((3, RA, width), bf),
         a_recv=v((5, RA, width), bf),
-        b_send=v((4, SUPER, width), bf),
+        b_send=v((3, SUPER, width), bf),
         b_recv=v((5, SUPER, width), bf),
         bh_send=v((RB, width), bf),
         bh_recv=v((2, HB, width), bf),
@@ -418,13 +417,221 @@
         g2_recv=pltpu.SemaphoreType.DMA((6, 2, 4)),
         rs_send=pltpu.SemaphoreType.DMA((6, 2, 5)),
         rs_recv=pltpu.SemaphoreType.DMA((6, 2, 5)),
-        local=pltpu.SemaphoreType.DMA((5,)),
+        local=pltpu.SemaphoreType.DMA((7,)),
+        d_send=v((2, 2, HALF, hidden, rows), bf),
+        d_recv=v((2, 2, HALF, hidden, rows), bf),
+        z_send=v((2, modules, hidden, rows), bf),
+        z_recv=v((2, modules, hidden, rows), bf),
+        fresh=v((2, modules, hidden, rows), bf),
+        far_0=v((modules, hidden, rows), bf),
+        far_1=v((modules, hidden, rows), bf),
+        mast=v((2, modules, hidden, rows), f32),
+        mom=v((2, modules, hidden, rows), f32),
+        ds=pltpu.SemaphoreType.DMA((2, 2, HALF)),
+        dr=pltpu.SemaphoreType.DMA((2, 2, HALF)),
+        os=pltpu.SemaphoreType.DMA((2, 2, HALF)),
+        orv=pltpu.SemaphoreType.DMA((2, 2, HALF)),
+        zs=pltpu.SemaphoreType.DMA((2, 2)),
+        zr=pltpu.SemaphoreType.DMA((2, 2)),
+        out=pltpu.SemaphoreType.DMA((2, 2)),
     )
 
 
-def step_kernel(names, width_scale, hidden_scale, tokens, x_ref, t_ref, keep_ref, w_ref, delta_ref, *refs):
+HALF = 8
+PATHS_PER_MODULE = 4
+
+
+class Group:
+    def __init__(self):
+        p = lax.axis_index("path")
+        self.h, self.i = p // HALF, p % HALF
+        self.y, self.c = self.i // 2, self.i % 2
+        self.across = (1 - self.h) * HALF + self.i
+
+    def peer(self, i):
+        return self.h * HALF + i
+
+
+def pcopy(src, dst, ssem, rsem, p):
+    return pltpu.make_async_remote_copy(
+        src_ref=src, dst_ref=dst, send_sem=ssem, recv_sem=rsem, device_id={"path": p}, device_id_type=MESH
+    )
+
+
+def path_phase(pg, sc, width_scale, hidden_scale, table, new_w, new_mast, new_mom):
+    h, me = pg.h, pg.i
+    hidden, rows = sc.mast.shape[2:]
+    modules = sc.mast.shape[1]
+    operands = ((sc.xg, sc.pre_grad, width_scale), (sc.og, sc.act, hidden_scale))
+
+    def half(side):
+        return h if side == 0 else 1 - h
+
+    def dcopy(level, side, i, src):
+        return pcopy(sc.d_send.at[level, side, i], sc.d_recv.at[level, side, src], sc.ds.at[level, side, i], sc.dr.at[level, side, src], pg.peer(i))
+
+    def changes(level, side):
+        left, right, scale = operands[level]
+
+        def run(k, c):
+            d = jnp.where(k == 0, 2, jnp.where(k == 1, 1, jnp.where(k == 2, 3, 0)))
+            y = (pg.y + d) % 4
+            cols = pl.ds(pl.multiple_of((half(side) * HALF + 2 * y) * rows, 128), 2 * rows)
+            g = lax.dot_general(right[...], left[:, cols], (((0,), (0,)), ((), ())), preferred_element_type=jnp.float32)
+            g = (INNER_LR * scale * g).astype(jnp.bfloat16)
+            for core in (0, 1):
+                i = 2 * y + core
+                part = g[:, core * rows : (core + 1) * rows]
+
+                @pl.when(i == me)
+                def _():
+                    sc.d_recv[level, side, i] = part
+
+                @pl.when(i != me)
+                def _():
+                    sc.d_send[level, side, i] = part
+                    dcopy(level, side, i, me).start()
+
+            return c
+
+        lax.fori_loop(0, 4, run, 0)
+
+    def await_changes(level, side):
+        def run(i, c):
+            @pl.when(i != me)
+            def _():
+                dcopy(level, side, i, i).wait_recv()
+
+            return c
+
+        lax.fori_loop(0, HALF, run, 0)
+
+    STEP = 32
+
+    def sums(level, side, use):
+        def run(k, c):
+            part = pl.ds(pl.multiple_of(k * STEP, STEP), STEP)
+            total = [jnp.zeros((STEP, rows), jnp.float32) for _ in range(modules)]
+            for i in range(HALF):
+                change = sc.d_recv[level, side, i, part, :].astype(jnp.float32)
+                named = table[pg.peer(i), level]
+                for m in range(modules):
+                    total[m] = total[m] + jnp.where(named == m, 1.0, 0.0) * change
+            for m in range(modules):
+                use(m, part, total[m])
+            return c
+
+        lax.fori_loop(0, hidden // STEP, run, 0)
+
+    far = (sc.far_0, sc.far_1)
+
+    def zcopy(kind, level):
+        src, dst = (sc.z_send.at[level], sc.z_recv.at[level]) if kind == 0 else (sc.fresh.at[level], far[level])
+        return pcopy(src, dst, sc.zs.at[kind, level], sc.zr.at[kind, level], pg.across)
+
+    def sums_across(level):
+        await_changes(level, 1)
+
+        def use(m, part, total):
+            sc.z_send[level, m, part, :] = total.astype(jnp.bfloat16)
+
+        sums(level, 1, use)
+        zcopy(0, level).start()
+
+    def outs(level):
+        return [
+            pltpu.make_async_copy(sc.mast.at[level], new_mast.at[level], sc.out.at[0, level]),
+            pltpu.make_async_copy(sc.mom.at[level], new_mom.at[level], sc.out.at[1, level]),
+        ]
+
+    def update(level):
+        await_changes(level, 0)
+        zcopy(0, level).wait_recv()
+
+        def use(m, part, total):
+            average = (total + sc.z_recv[level, m, part, :].astype(jnp.float32)) * (1.0 / PATHS_PER_MODULE)
+            moved = MOMENT * sc.mom[level, m, part, :] + average
+            master = sc.mast[level, m, part, :] - OUTER_LR * (average + MOMENT * moved)
+            sc.mom[level, m, part, :] = moved
+            sc.mast[level, m, part, :] = master
+            sc.fresh[level, m, part, :] = master.astype(jnp.bfloat16)
+
+        sums(level, 0, use)
+        zcopy(1, level).start()
+        for c in outs(level):
+            c.start()
+
+    def ocopy(level, side, i, src):
+        place = pl.ds(pl.multiple_of((half(side) * HALF + src) * rows, 128), rows)
+        return pcopy(sc.d_send.at[level, side, i], new_w.at[level, :, place], sc.os.at[level, side, i], sc.orv.at[level, side, src], pg.peer(i))
+
+    def own_copy(level, side):
+        place = pl.ds(pl.multiple_of((half(side) * HALF + me) * rows, 128), rows)
+        return pltpu.make_async_copy(sc.d_send.at[level, side, me], new_w.at[level, :, place], sc.os.at[level, side, me])
+
+    def hand_back(level, side):
+        if side == 1:
+            zcopy(1, level).wait_recv()
+
+        def run(k, c):
+            i = (me + 1 + k) % HALF
+
+            @pl.when(i != me)
+            def _():
+                dcopy(level, side, i, me).wait_send()
+
+            named = table[pg.peer(i), level]
+            sc.d_send[level, side, i] = sc.fresh[level, named] if side == 0 else far[level][named]
+
+            @pl.when(i != me)
+            def _():
+                ocopy(level, side, i, me).start()
+
+            @pl.when(i == me)
+            def _():
+                own_copy(level, side).start()
+
+            return c
+
+        lax.fori_loop(0, HALF, run, 0)
+
+    changes(1, 1)
+    changes(0, 1)
+    changes(1, 0)
+    sums_across(1)
+    changes(0, 0)
+    sums_across(0)
+    update(1)
+    hand_back(1, 0)
+    update(0)
+    hand_back(0, 0)
+    hand_back(1, 1)
+    hand_back(0, 1)
+
+    for level in (0, 1):
+        for side in (0, 1):
+            own_copy(level, side).wait()
+
+            def drain(i, c):
+                @pl.when(i != me)
+                def _():
+                    ocopy(level, side, i, i).wait_recv()
+                    ocopy(level, side, i, me).wait_send()
+
+                return c
+
+            lax.fori_loop(0, HALF, drain, 0)
+        zcopy(0, level).wait_send()
+        zcopy(1, level).wait_send()
+        for c in outs(level):
+            c.wait()
+
+
+def step_kernel(names, width_scale, hidden_scale, tokens, x_ref, t_ref, keep_ref, table_ref, w_ref, mast_ref, mom_ref,
+                new_w_ref, new_mast_ref, new_mom_ref, *refs):
     sc = Refs(**dict(zip(names, refs)))
     pp = Place()
+    pg = Group()
     x, z, w = pp.x, pp.z, pp.w
     own_a, own_b = rows_a(x, z), rows_b(x, z)
 
@@ -434,6 +641,8 @@
         pltpu.make_async_copy(w_ref.at[0], sc.w_in, sc.local.at[2]),
         pltpu.make_async_copy(w_ref.at[1], sc.w_out, sc.local.at[3]),
         pltpu.make_async_copy(t_ref, sc.tgt, sc.local.at[4]),
+        pltpu.make_async_copy(mast_ref, sc.mast, sc.local.at[5]),
+        pltpu.make_async_copy(mom_ref, sc.mom, sc.local.at[6]),
     ]
     for c in loads:
         c.start()
@@ -446,24 +655,31 @@
     def _():
         pl.semaphore_signal(barrier, inc=1, device_id={"fsdp": pp.edge}, device_id_type=MESH)
 
-    pl.semaphore_wait(barrier, 3 + w)
+    for i in range(HALF):
+
+        @pl.when(pg.i != i)
+        def _():
+            pl.semaphore_signal(barrier, inc=1, device_id={"path": pg.peer(i)}, device_id_type=MESH)
+
+    pl.semaphore_signal(barrier, inc=1, device_id={"path": pg.across}, device_id_type=MESH)
+    pl.semaphore_wait(barrier, 3 + HALF + w)
     for c in loads:
         c.wait()
 
+    def across_width(rows, weights):
+        return lax.dot_general(rows, weights[...], (((1,), (1,)), ((), ())), preferred_element_type=jnp.float32)
+
     def forward(start, n):
         rows = pl.ds(start, n)
-        pre = jnp.dot(sc.xg[rows, :], sc.w_in[...], preferred_element_type=jnp.float32) * width_scale
+        pre = across_width(sc.xg[rows, :], sc.w_in) * width_scale
         sig = jax.nn.sigmoid(pre)
         sc.act[rows, :] = (pre * sig).astype(jnp.bfloat16)
         sc.slope[rows, :] = sig * (1.0 + pre * (1.0 - sig))
 
     gather(pp, sc.xg, sc.g1_send, sc.g1_recv, forward)
 
-    for k in range(0, sc.w_out.shape[0], 256):
-        sc.w_out_t[:, k : k + 256] = sc.w_out[k : k + 256, :].T
-
     def partial(start, n, cs):
-        return jnp.dot(sc.act[pl.ds(start, n), :], sc.w_out_t[:, cs], preferred_element_type=jnp.float32) * hidden_scale
+        return jnp.dot(sc.act[pl.ds(start, n), :], sc.w_out[:, cs], preferred_element_type=jnp.float32) * hidden_scale
 
     reduce(pp, partial, sc)
 
@@ -476,24 +692,16 @@
 
     def backward(start, n):
         rows = pl.ds(start, n)
-        act_grad = jnp.dot(sc.og[rows, :], sc.w_out[...], preferred_element_type=jnp.float32) * hidden_scale
+        act_grad = across_width(sc.og[rows, :], sc.w_out) * hidden_scale
         sc.pre_grad[rows, :] = (act_grad * sc.slope[rows, :]).astype(jnp.bfloat16)
 
     gather(pp, sc.og, sc.g2_send, sc.g2_recv, backward)
 
-    def grads(level, left, right, scale):
-        def run(k, c):
-            cols = pl.ds(pl.multiple_of(k * 256, 256), 256)
-            g = lax.dot_general(
-                left[:, cols], right[...], (((0,), (0,)), ((), ())), preferred_element_type=jnp.float32
-            )
-            delta_ref[level, cols, :] = (INNER_LR * scale * g).astype(jnp.bfloat16)
-            return c
-
-        lax.fori_loop(0, left.shape[1] // 256, run, 0)
-
-    grads(1, sc.og, sc.act, hidden_scale)
-    grads(0, sc.xg, sc.pre_grad, width_scale)
+    path_phase(pg, sc, width_scale, hidden_scale, table_ref, new_w_ref, new_mast_ref, new_mom_ref)
+
+
+def turn(v):
+    return jnp.swapaxes(v, -1, -2)
 
 
 def per_device(inputs, targets, token_ids, module_table, path_weights, master, momentum):
@@ -501,37 +709,27 @@
     n = lax.axis_size("fsdp")
     tokens = inputs.shape[1] * n
     keep = (token_ids[0] >= SPECIAL).astype(jnp.float32)[:, None]
-    spec = scratch(width, hidden)
+    modules, rows = master.shape[1:3]
+    spec = scratch(width, hidden, modules, rows)
     hbm = pl.BlockSpec(memory_space=pl.ANY)
     vmem = pl.BlockSpec(memory_space=pltpu.VMEM)
-    delta = pl.pallas_call(
+    smem = pl.BlockSpec(memory_space=pltpu.SMEM)
+    new_weights, new_master, new_momentum = pl.pallas_call(
         functools.partial(step_kernel, tuple(spec), width ** (-0.5), (hidden * n) ** (-0.5), tokens),
-        out_shape=jax.ShapeDtypeStruct((2, width, hidden), jnp.bfloat16),
-        in_specs=[hbm, hbm, vmem, hbm],
-        out_specs=vmem,
+        out_shape=(
+            jax.ShapeDtypeStruct((2, hidden, width), jnp.bfloat16),
+            jax.ShapeDtypeStruct((2, modules, hidden, rows), jnp.float32),
+            jax.ShapeDtypeStruct((2, modules, hidden, rows), jnp.float32),
+        ),
+        in_specs=[hbm, hbm, vmem, smem, hbm, hbm, hbm],
+        out_specs=(hbm, hbm, hbm),
         scratch_shapes=list(spec.values()),
         compiler_params=pltpu.CompilerParams(
-            collective_id=0, has_side_effects=True, vmem_limit_bytes=62 * 1024 * 1024
+            collective_id=0, has_side_effects=True, vmem_limit_bytes=63 * 1024 * 1024
         ),
-        name="inner_step",
-    )(inputs[0], targets[0], keep, path_weights[0])
-
-    arrived = lax.all_to_all(delta[:, None], "path", split_axis=2, concat_axis=1, tiled=True).astype(jnp.float32)
-    modules = master.shape[1]
-    labels = jnp.arange(modules, dtype=jnp.int32)
-    pick = (module_table.T[:, None, :] == labels[None, :, None]).astype(jnp.float32)
-    counts = jnp.sum(pick, axis=2)
-    sums = jnp.einsum("lmq,lqrc->lmrc", pick, arrived, precision=lax.Precision.HIGHEST)
-    average = sums / counts[:, :, None, None]
-    new_momentum = MOMENT * momentum + average
-    new_master = master - OUTER_LR * (average + MOMENT * new_momentum)
-    route = jnp.transpose(pick, (0, 2, 1)).astype(jnp.bfloat16)
-    outgoing = jnp.einsum(
-        "lqm,lmrc->lqrc", route, new_master.astype(jnp.bfloat16), preferred_element_type=jnp.float32
-    ).astype(jnp.bfloat16)
-    returned = lax.all_to_all(outgoing, "path", split_axis=1, concat_axis=2, tiled=True)
-    new_weights = jnp.transpose(returned, (1, 0, 2, 3))
-    return (new_weights, new_master, new_momentum)
+        name="outer_step",
+    )(inputs[0], targets[0], keep, module_table, turn(path_weights[0]), turn(master), turn(momentum))
+    return (turn(new_weights)[None], turn(new_master), turn(new_momentum))
 
 
 def solution(mesh):

time: 410 us -> 316 us (0.77)
  waiting for transfers between devices: 120 us -> 0 us
  Pallas kernels: 218 us -> 300 us
  local copies, waits for them, and re-layouts: 34.8 us -> 8.95 us
  starting transfers between devices: 21.5 us -> 0 us
  matrix products: 7.59 us -> 0 us
    all_to_all x2 -> x0, waiting for transfers between devices: 120 us -> none  [the longest x1 79.6 us: per_device(): lax.all_to_all(delta[:, None], 'path', split_axis=2, concat_axis=1, tiled...]
    pallas_call x1, Pallas kernels: 218 us -> 300 us  [per_device(): pl.pallas_call(functools.partial(step_kernel, tuple(spec), width ** (-0.5...]
    all_to_all x2 -> x0, starting transfers between devices: 21.5 us -> none  [the longest x1 16.9 us: per_device(): lax.all_to_all(delta[:, None], 'path', split_axis=2, concat_axis=1, tiled...]
    all_to_all x2 -> x0, local copies, waits for them, and re-layouts: 8.57 us -> none  [the longest x1 5.13 us: per_device(): lax.all_to_all(delta[:, None], 'path', split_axis=2, concat_axis=1, tiled...]
    broadcast_in_dim x1 -> x0, local copies, waits for them, and re-layouts: 8.01 us -> none  [per_device(): delta[:, None]]
    dot_general x2 -> x0, matrix products: 7.59 us -> none  [the longest x1 6.32 us: per_device(): jnp.einsum('lmq,lqrc->lmrc', pick, arrived, precision=lax.Precision.HIGHEST)]
    transpose x1 -> x0, local copies, waits for them, and re-layouts: 5.53 us -> none  [per_device(): new_weights = jnp.transpose(returned, (1, 0, 2, 3))]
    unnamed x9 -> x8, local copies, waits for them, and re-layouts: 9.6 us -> 8.21 us
  transfers between devices with their start and end apart: 2 -> 0, of which waited for: 2 -> 0; matrix products, arithmetic and copies ran while one was open for 1% -> 0% of each run, Pallas kernels for 0% -> 0%
where the time goes in v2:
time: 316 us; the launch traced here: 310 us
  Pallas kernels  300 us (95%)
  local copies, waits for them, and re-layouts  8.95 us (3%)
    pallas_call x1, Pallas kernels, per_device(): pl.pallas_call(functools.partial(step_kernel, tuple(spec), width ** (-0.5...  300 us
    unnamed x8, local copies, waits for them, and re-layouts  8.21 us

profile of v2, /device:TPU:121, one launch (start us, length us, event | category | flops | bytes accessed | tf_op | source)
XLA Modules:
  0.0 310.2 jit_solution(7482512547558896553)
XLA Ops:
  0.6 0.7 fusion
  1.3 1.4 copy.11.table_ref
  2.6 0.7 copy.10.keep_ref
  3.4 300.0 %outer_step.1 = (bf16[2,352,2048]{2,1,0:T(8,128)(2,1)}, f32[2,4,352,128]{3,2,1,0:T(8,128)}, f32[2,4,352,128]{3,2,1,0:T(8,128)}) custom-call(bf16[128,2048]{1,0:T(8,128)(2,1)} %bitcast.20, bf16[128,2048]{1,0:T(8,128)(2,1)} %bitcast.21, f32[128,1]{1,0:T(8,128)} %copy.10.keep_ref, s32[16,2]{1,0:T(8,128)} %copy.11.table_ref, bf16[2,352,2048]{2,1,0:T(8,128)(2,1)} %bitcast.14, ...), custom_call_target="tpu_custom_call" | custom-call | tf_op jit(solution)/shard_map/outer_step/pallas_call | solution.py:717
  303.4 0.0 copy-start.1
  303.4 3.9 %copy.15 = bf16[1,2,2048,352]{2,3,1,0:T(8,128)(2,1)} copy(bf16[1,2,2048,352]{2,3,1,0:T(8,128)(2,1)} %bitcast.15) | data formatting | bytes 5767168
  307.2 0.0 copy-done.1
  307.2 0.0 copy-start
  307.2 1.1 copy.16
  308.3 0.8 copy-done
  309.1 1.1 copy.17
Async XLA Ops:
  303.4 3.9 %copy-start.1 = (f32[2,4,352,128]{3,2,1,0:T(8,128)S(1)}, f32[2,4,352,128]{3,2,1,0:T(8,128)}, u32[]{:S(2)}) copy-start(f32[2,4,352,128]{3,2,1,0:T(8,128)} %get-tuple-element.7) | copy-start | bytes 4325380
  307.2 1.9 copy-start

commit v3 on v0

v3 whole, which is shorter than its diff:
```python
import functools

import jax
import jax.numpy as jnp
from jax import lax
from jax.experimental import pallas as pl
from jax.experimental.pallas import tpu as pltpu
from jax.sharding import PartitionSpec as P

SPECIAL = 256
INNER_LR = 4096.0
OUTER_LR = 0.7
MOMENT = 0.9
MESH = pl.DeviceIdType.MESH

CHUNKS = 2
RA, RB = 48, 16
NX, NZ = 4, 4
LINE = NX * RA
SUPER = NX * RB
ROWS_A = NZ * LINE
CHUNK = ROWS_A + NZ * SUPER
OWN = RA + RB


class Place:
    def __init__(self):
        f = lax.axis_index("fsdp")
        self.x, self.z = f // NZ, f % NZ
        self.far = self.z // 2
        self.w = (self.z + self.far) % 2
        flip = 1 - 2 * self.far
        self.flip = flip
        self.right = ((self.x + 1) % NX) * NZ + self.z
        self.left = ((self.x + NX - 1) % NX) * NZ + self.z
        self.inner = self.x * NZ + self.z + flip
        self.edge = self.x * NZ + self.z - flip

    def zb(self, r):
        swap = jnp.where(r == 0, 1, jnp.where(r == 1, -1, 0))
        o = r + self.w * swap
        return o * self.flip + (NZ - 1) * self.far

    def col(self, dx):
        return (self.x + dx + NX) % NX


def rows_line(c, z):
    return pl.multiple_of(c * CHUNK + z * LINE, 16)


def rows_a(c, x, z):
    return pl.multiple_of(c * CHUNK + z * LINE + x * RA, 16)


def rows_b(c, x, z):
    return pl.multiple_of(c * CHUNK + ROWS_A + z * SUPER + x * RB, 16)


def rows_super(c, z):
    return pl.multiple_of(c * CHUNK + ROWS_A + z * SUPER, 16)


def rcopy(src, dst, ssem, rsem, f):
    return pltpu.make_async_remote_copy(
        src_ref=src, dst_ref=dst, send_sem=ssem, recv_sem=rsem, device_id={"fsdp": f}, device_id_type=MESH
    )


STEPS = 6


class Gather:
    FIRST = (0, 4, 12, 20, 22, 24)
    PER_SIDE = (4, 4, 4, 1, 1, 4)
    RECV = 28

    def __init__(self, pp, chunk, buf, ssem, rsem, compute):
        self.pp, self.chunk, self.buf, self.ssem, self.rsem, self.compute = pp, chunk, buf, ssem, rsem, compute
        self.half = buf.shape[1] // 2

    def piece(self, start, n, side=None):
        if side is None:
            return self.buf.at[pl.ds(start, n)]
        return self.buf.at[pl.ds(start, n), pl.ds(side * self.half, self.half)]

    def copy(self, kind, side, i, ref, f, slot):
        c = self.chunk
        got = self.FIRST[kind] + slot[0] * self.PER_SIDE[kind] + slot[1]
        return rcopy(ref, ref, self.ssem.at[c, kind], self.rsem.at[c, got], f)

    def push(self, kind, side, i, ref, f, slot):
        self.copy(kind, side, i, ref, f, slot).start()

    def arrived(self, kind, side, i, ref):
        self.copy(kind, side, i, ref, self.pp.right, (side, i)).wait_recv()

    def sent(self, kind, n):
        self.copy(kind, 0, 0, self.piece(0, n), self.pp.right, (0, 0)).wait_send()

    def z_own(self, kind, ref):
        pp = self.pp
        self.push(kind, 0, 0, ref, pp.inner, (0, pp.z))

        @pl.when(pp.w == 1)
        def _():
            self.push(kind, 1, 0, ref, pp.edge, (0, pp.z))

    def z_forward(self, kind, r, zb, ref):
        pp = self.pp

        @pl.when((pp.w == 1) & (r == 1))
        def _():
            self.push(kind, 0, r, ref, pp.inner, (0, zb))

        @pl.when((pp.w == 1) & (r >= 2))
        def _():
            self.push(kind, 1, r, ref, pp.edge, (0, zb))

    def start(self):
        pp, c = self.pp, self.chunk
        self.z_own(0, self.piece(rows_a(c, pp.x, pp.z), RA))
        for side, f in ((0, pp.right), (1, pp.left)):
            self.push(3, side, 0, self.piece(rows_b(c, pp.x, pp.z), RB), f, (side, 0))

    def step(self, t):
        pp, c = self.pp, self.chunk
        z = pp.z
        sides = ((0, -1, pp.right), (1, 1, pp.left))
        zt, zl = pp.zb(t), pp.zb(t - 1)

        @pl.when((t >= 1) & (t <= 3))
        def _():
            ref = self.piece(rows_a(c, pp.x, zt), RA)
            self.arrived(0, 0, zt, ref)
            self.z_forward(0, t, zt, ref)

        @pl.when(t <= 3)
        def _():
            for side, _, f in sides:
                self.push(1, side, t, self.piece(rows_a(c, pp.x, zt), RA), f, (side, t))

        @pl.when(t == 0)
        def _():
            for side, dx, f in sides:
                start = rows_b(c, pp.col(dx), z)
                self.arrived(3, side, 0, self.piece(start, RB))
                self.push(4, side, 0, self.piece(start, RB, side), f, (side, 0))

        @pl.when((t >= 1) & (t <= 4))
        def _():
            for side, dx, f in sides:
                start = rows_a(c, pp.col(dx), zl)
                self.arrived(1, side, t - 1, self.piece(start, RA))
                self.push(2, side, t - 1, self.piece(start, RA, side), f, (side, t - 1))

        @pl.when(t == 1)
        def _():
            for side in (0, 1):
                self.arrived(4, side, 0, self.piece(rows_b(c, pp.col(2), z), RB, side))
            self.z_own(5, self.piece(rows_super(c, z), SUPER))

        @pl.when((t >= 2) & (t <= 4))
        def _():
            ref = self.piece(rows_super(c, zl), SUPER)
            self.arrived(5, 0, zl, ref)
            self.z_forward(5, t - 1, zl, ref)

        @pl.when((t >= 1) & (t <= 4))
        def _():
            self.compute(rows_super(c, zl), SUPER)

        @pl.when(t >= 2)
        def _():
            zo = pp.zb(t - 2)
            for side in (0, 1):
                self.arrived(2, side, t - 2, self.piece(rows_a(c, pp.col(2), zo), RA, side))
            self.compute(rows_line(c, zo), LINE)

    def finish(self):
        for kind, n in ((0, RA), (5, SUPER)):

            @pl.when(self.pp.w == 0)
            def _():
                self.sent(kind, n)

            @pl.when(self.pp.w == 1)
            def _():
                self.sent(kind, 5 * n)

        for kind, n in ((1, 8 * RA), (2, 4 * RA), (3, 2 * RB), (4, RB)):
            self.sent(kind, n)


COLS = 512


def up(v):
    return v.astype(jnp.float32)


class Reduce:
    def __init__(self, pp, chunk, partial, sc):
        self.pp, self.chunk, self.partial, self.sc = pp, chunk, partial, sc
        self.width = sc.acc_a.shape[-1]

    def over(self, body, first=0, width=None):
        def run(k, carry):
            body(pl.ds(pl.multiple_of(first + k * COLS, 128), COLS))
            return carry

        lax.fori_loop(0, (width or self.width) // COLS, run, 0)

    FIRST = (0, 8, 16, 18, 23, 28)
    PER_SIDE = (4, 4, 1, 5, 5, 1)
    RECV = 30

    def copy(self, src, dst, kind, side, i, f, slot):
        c, sc = self.chunk, self.sc
        got = self.FIRST[kind] + slot[0] * self.PER_SIDE[kind] + slot[1]
        return rcopy(src, dst, sc.rs_send.at[c, kind], sc.rs_recv.at[c, got], f)

    def push(self, src, dst, kind, side, i, f, slot):
        self.copy(src, dst, kind, side, i, f, slot).start()

    def arrived(self, ref, kind, side, i):
        self.copy(ref, ref, kind, side, i, self.pp.right, (side, i)).wait_recv()

    def sent(self, ref, kind):
        self.copy(ref, ref, kind, 0, 0, self.pp.right, (0, 0)).wait_send()

    def z_stage(self, kind, r, acc, recv, send):
        pp, c, w = self.pp, self.chunk, self.pp.w

        @pl.when((w == 1) & (r >= 1))
        def _():
            self.arrived(recv.at[c, r], kind, 0, r)

            def add(cs):
                send[c, r - 1, :, cs] = (acc[c, :, cs] + up(recv[c, r, :, cs])).astype(jnp.bfloat16)

            self.over(add)

        @pl.when((w == 1) & (r >= 2))
        def _():
            slot = jnp.where(r == 3, 1, 0)
            self.push(send.at[c, r - 1], recv.at[c, slot], kind, 0, r, pp.inner, (0, slot))

        @pl.when((w == 1) & (r == 1))
        def _():
            self.push(send.at[c, r - 1], recv.at[c, 0], kind, 0, r, pp.edge, (0, 0))

        @pl.when((w == 0) & (r >= 1))
        def _():
            def cast(cs):
                send[c, r - 1, :, cs] = acc[c, :, cs].astype(jnp.bfloat16)

            self.over(cast)
            slot = jnp.where(r == 1, 4, r)
            self.push(send.at[c, r - 1], recv.at[c, slot], kind, 0, r, pp.inner, (0, slot))

        def last(i):
            self.arrived(recv.at[c, i], kind, 0, i)

            def add(cs):
                acc[c, :, cs] = acc[c, :, cs] + up(recv[c, i, :, cs])

            self.over(add)

        @pl.when(r == 0)
        def _():
            last(0)

        @pl.when((w == 1) & (r == 0))
        def _():
            last(4)

    def b_round(self, r):
        sc, c = self.sc, self.chunk
        start = rows_super(c, self.pp.zb(r))

        def fill(cs):
            sc.acc_b[c, :, cs] = self.partial(start, SUPER, cs)

        self.over(fill)
        self.z_stage(4, r, sc.acc_b, sc.b_recv, sc.b_send)

    def step(self, t):
        pp, sc, c, w = self.pp, self.sc, self.chunk, self.pp.w
        r0, r1, r2 = 3 - t, 4 - t, 5 - t
        half = self.width // 2

        def rows(dx, n):
            return pl.ds(pl.multiple_of(pp.col(dx) * n, 16), n)

        sides = ((0, 1, pp.right, half), (1, -1, pp.left, 0))

        @pl.when(t <= 3)
        def _():
            start = rows_line(c, pp.zb(r0))

            def fill(cs):
                sc.part[c, r0, :, cs] = self.partial(start, LINE, cs).astype(jnp.bfloat16)

            self.over(fill)
            for side, _, f, lo in sides:
                src = sc.part.at[c, r0, rows(2, RA), pl.ds(lo, half)]
                self.push(src, sc.h_recv.at[c, side, r0], 0, side, r0, f, (side, r0))

        @pl.when((t == 0) & (w == 0))
        def _():
            def run(i, carry):
                self.b_round(3 - i)
                return carry

            lax.fori_loop(0, 3, run, 0)

        @pl.when((t >= 1) & (t <= 4))
        def _():
            for side, dx, f, lo in sides:
                self.arrived(sc.h_recv.at[c, side, r1], 0, side, r1)
                where = rows(dx, RA)

                def add(cs):
                    to = pl.ds(pl.multiple_of(lo + cs.start, 128), COLS)
                    sc.part[c, r1, where, to] = (up(sc.part[c, r1, where, to]) + up(sc.h_recv[c, side, r1, :, cs])).astype(jnp.bfloat16)

                self.over(add, width=half)
                self.push(sc.part.at[c, r1, where], sc.f_recv.at[c, side, r1], 1, side, r1, f, (side, r1))

        @pl.when((t >= 1) & (t <= 3) & (w == 1))
        def _():
            self.b_round(r1)

        @pl.when(t == 4)
        def _():
            self.b_round(0)
            sc.bh_send[c] = sc.acc_b[c, rows(2, RB), :].astype(jnp.bfloat16)
            for side, _, f, lo in sides:
                self.push(sc.bh_send.at[c, :, pl.ds(lo, half)], sc.bh_recv.at[c, side], 2, side, 0, f, (side, 0))

        @pl.when(t >= 2)
        def _():
            for side in (0, 1):
                self.arrived(sc.f_recv.at[c, side, r2], 1, side, r2)
            where = rows(0, RA)

            def fill(cs):
                sc.acc_a[c, :, cs] = up(sc.part[c, r2, where, cs]) + up(sc.f_recv[c, 0, r2, :, cs]) + up(sc.f_recv[c, 1, r2, :, cs])

            self.over(fill)
            self.z_stage(3, r2, sc.acc_a, sc.a_recv, sc.a_send)

        @pl.when(t == 4)
        def _():
            for side, dx, f, lo in sides:
                self.arrived(sc.bh_recv.at[c, side], 2, side, 0)
                where = rows(dx, RB)
                got, alone = pl.ds(lo, half), pl.ds(half - lo, half)
                sc.bf_send[c, side, :, got] = (sc.acc_b[c, where, got] + up(sc.bh_recv[c, side])).astype(jnp.bfloat16)
                sc.bf_send[c, side, :, alone] = sc.acc_b[c, where, alone].astype(jnp.bfloat16)
                self.push(sc.bf_send.at[c, side], sc.bf_recv.at[c, side], 5, side, 0, f, (side, 0))

    def finish(self):
        pp, sc, c = self.pp, self.sc, self.chunk
        for side in (0, 1):
            self.arrived(sc.bf_recv.at[c, side], 5, side, 0)
        own = pl.multiple_of(pp.x * RB, 16)
        sc.fin_b[...] = sc.acc_b[c, pl.ds(own, RB), :] + up(sc.bf_recv[c, 0]) + up(sc.bf_recv[c, 1])

    def drain(self):
        sc, c = self.sc, self.chunk
        sent = ((sc.h_recv, 0), (sc.f_recv, 1), (sc.bh_recv, 2), (sc.a_send, 3), (sc.b_send, 4), (sc.bf_recv, 5))
        for ref, kind in sent:
            self.sent(ref.at[c], kind)


class Refs:
    def __init__(self, **kw):
        self.__dict__.update(kw)


def scratch(width, hidden, modules, rows):
    bf, f32 = jnp.bfloat16, jnp.float32
    tokens = CHUNKS * CHUNK
    v = pltpu.VMEM
    return dict(
        xg=v((tokens, width), bf),
        og=v((tokens, width), bf),
        w_in=v((hidden, width), bf),
        w_out=v((hidden, width), bf),
        act=v((tokens, hidden), bf),
        slope=v((tokens, hidden), f32),
        pre_grad=v((tokens, hidden), bf),
        tgt=v((CHUNKS * OWN, width), bf),
        keep=v((CHUNKS * OWN, CHUNKS * OWN), f32),
        part=v((CHUNKS, 4, LINE, width), bf),
        h_recv=v((CHUNKS, 2, 4, RA, width // 2), bf),
        f_recv=v((CHUNKS, 2, 4, RA, width), bf),
        a_send=v((CHUNKS, 3, RA, width), bf),
        a_recv=v((CHUNKS, 5, RA, width), bf),
        b_send=v((CHUNKS, 3, SUPER, width), bf),
        b_recv=v((CHUNKS, 5, SUPER, width), bf),
        bh_send=v((CHUNKS, RB, width), bf),
        bh_recv=v((CHUNKS, 2, RB, width // 2), bf),
        bf_send=v((CHUNKS, 2, RB, width), bf),
        bf_recv=v((CHUNKS, 2, RB, width), bf),
        acc_a=v((CHUNKS, RA, width), f32),
        acc_b=v((CHUNKS, SUPER, width), f32),
        fin_b=v((RB, width), f32),
        g_send=pltpu.SemaphoreType.DMA((CHUNKS, 6)),
        g_recv=pltpu.SemaphoreType.DMA((CHUNKS, Gather.RECV)),
        rs_send=pltpu.SemaphoreType.DMA((CHUNKS, 6)),
        rs_recv=pltpu.SemaphoreType.DMA((CHUNKS, Reduce.RECV)),
        local=pltpu.SemaphoreType.DMA((5,)),
        own=pltpu.SemaphoreType.DMA((CHUNKS, 2)),
        d_send=v((2, 2, HALF, hidden, rows), bf),
        d_recv=v((2, 2, HALF, hidden, rows), bf),
        z_send=v((2, modules, hidden, rows), bf),
        z_recv=v((2, modules, hidden, rows), bf),
        fresh=v((2, modules, hidden, rows), bf),
        far_00=v((modules, SPLIT, rows), bf),
        far_01=v((modules, hidden - SPLIT, rows), bf),
        far_10=v((modules, SPLIT, rows), bf),
        far_11=v((modules, hidden - SPLIT, rows), bf),
        mast=v((2, modules, hidden, rows), f32),
        mom=v((2, modules, hidden, rows), f32),
        ds=pltpu.SemaphoreType.DMA((2, 2, PIECES)),
        dr=pltpu.SemaphoreType.DMA((2, 2, PIECES)),
        os=pltpu.SemaphoreType.DMA((2, 2, PIECES)),
        orv=pltpu.SemaphoreType.DMA((2, 2, PIECES)),
        own_out=pltpu.SemaphoreType.DMA((2, 2, PIECES)),
        zs=pltpu.SemaphoreType.DMA((2, 2, PIECES)),
        zr=pltpu.SemaphoreType.DMA((2, 2, PIECES)),
        out=pltpu.SemaphoreType.DMA((2, 2, PIECES)),
    )


HALF = 8
SPLIT = 128
PIECES = 2
PATHS_PER_MODULE = 4


class Group:
    def __init__(self):
        p = lax.axis_index("path")
        self.h, self.i = p // HALF, p % HALF
        self.y, self.c = self.i // 2, self.i % 2
        self.across = (1 - self.h) * HALF + self.i

    def peer(self, i):
        return self.h * HALF + i


def pcopy(src, dst, ssem, rsem, p):
    return pltpu.make_async_remote_copy(
        src_ref=src, dst_ref=dst, send_sem=ssem, recv_sem=rsem, device_id={"path": p}, device_id_type=MESH
    )


def path_phase(pg, sc, width_scale, hidden_scale, table, new_w, new_mast, new_mom):
    h, me = pg.h, pg.i
    hidden, rows = sc.mast.shape[2:]
    modules = sc.mast.shape[1]
    operands = ((sc.xg, sc.pre_grad, width_scale), (sc.og, sc.act, hidden_scale))

    def half(side):
        return h if side == 0 else 1 - h

    STEP = 32
    pieces = ((0, SPLIT), (SPLIT, hidden - SPLIT))

    def units(piece):
        return pl.ds(*pieces[piece])

    def dcopy(level, side, piece, i, src):
        return pcopy(
            sc.d_send.at[level, side, i, units(piece)],
            sc.d_recv.at[level, side, src, units(piece)],
            sc.ds.at[level, side, piece],
            sc.dr.at[level, side, piece],
            pg.peer(i),
        )

    def changes(level, side, which):
        left, right, scale = operands[level]
        first = pieces[which[0]][0]
        count = sum(pieces[piece][1] for piece in which)

        def run(k, c):
            d = jnp.where(k == 0, 2, jnp.where(k == 1, 1, jnp.where(k == 2, 3, 0)))
            y = (pg.y + d) % 4
            cols = pl.ds(pl.multiple_of((half(side) * HALF + 2 * y) * rows, 128), 2 * rows)
            g = lax.dot_general(
                right[:, first : first + count], left[:, cols], (((0,), (0,)), ((), ())), preferred_element_type=jnp.float32
            )
            g = (INNER_LR * scale * g).astype(jnp.bfloat16)
            for core in (0, 1):
                i = 2 * y + core
                part = g[:, core * rows : (core + 1) * rows]

                @pl.when(i == me)
                def _():
                    sc.d_recv[level, side, i, pl.ds(first, count), :] = part

                @pl.when(i != me)
                def _():
                    sc.d_send[level, side, i, pl.ds(first, count), :] = part
                    for piece in which:
                        dcopy(level, side, piece, i, me).start()

            return c

        lax.fori_loop(0, 4, run, 0)

    def all_dcopies(level, side, piece):
        ref = sc.d_recv.at[level, side, pl.ds(0, HALF - 1), units(piece)]
        return pcopy(ref, ref, sc.ds.at[level, side, piece], sc.dr.at[level, side, piece], pg.across)

    def await_changes(level, side, piece):
        all_dcopies(level, side, piece).wait_recv()

    def sums(level, side, piece, use):
        def run(k, c):
            part = pl.ds(pl.multiple_of(pieces[piece][0] + k * STEP, STEP), STEP)
            total = [jnp.zeros((STEP, rows), jnp.float32) for _ in range(modules)]
            for i in range(HALF):
                change = sc.d_recv[level, side, i, part, :].astype(jnp.float32)
                named = table[level, pg.peer(i)]
                for m in range(modules):
                    total[m] = total[m] + jnp.where(named == m, 1.0, 0.0) * change
            for m in range(modules):
                use(m, part, total[m])
            return c

        lax.fori_loop(0, pieces[piece][1] // STEP, run, 0)

    far = ((sc.far_00, sc.far_01), (sc.far_10, sc.far_11))

    def zcopy(kind, level, piece):
        src = (sc.z_send, sc.fresh)[kind].at[level, :, units(piece)]
        dst = far[level][piece] if kind else sc.z_recv.at[level, :, units(piece)]
        return pcopy(src, dst, sc.zs.at[kind, level, piece], sc.zr.at[kind, level, piece], pg.across)

    def sums_across(level, piece):
        await_changes(level, 1, piece)

        def use(m, part, total):
            sc.z_send[level, m, part, :] = total.astype(jnp.bfloat16)

        sums(level, 1, piece, use)
        zcopy(0, level, piece).start()

    def outs(level, piece):
        where = (level, slice(None), units(piece))
        return [
            pltpu.make_async_copy(sc.mast.at[where], new_mast.at[where], sc.out.at[0, level, piece]),
            pltpu.make_async_copy(sc.mom.at[where], new_mom.at[where], sc.out.at[1, level, piece]),
        ]

    def update(level, piece):
        await_changes(level, 0, piece)
        zcopy(0, level, piece).wait_recv()

        def use(m, part, total):
            average = (total + sc.z_recv[level, m, part, :].astype(jnp.float32)) * (1.0 / PATHS_PER_MODULE)
            moved = MOMENT * sc.mom[level, m, part, :] + average
            master = sc.mast[level, m, part, :] - OUTER_LR * (average + MOMENT * moved)
            sc.mom[level, m, part, :] = moved
            sc.mast[level, m, part, :] = master
            sc.fresh[level, m, part, :] = master.astype(jnp.bfloat16)

        sums(level, 0, piece, use)
        zcopy(1, level, piece).start()
        for c in outs(level, piece):
            c.start()

    def ocopy(level, side, piece, i, src):
        place = pl.ds(pl.multiple_of((half(side) * HALF + src) * rows, 128), rows)
        return pcopy(
            sc.d_send.at[level, side, i, units(piece)],
            new_w.at[level, units(piece), place],
            sc.os.at[level, side, piece],
            sc.orv.at[level, side, piece],
            pg.peer(i),
        )

    def own_copy(level, side, piece):
        place = pl.ds(pl.multiple_of((half(side) * HALF + me) * rows, 128), rows)
        return pltpu.make_async_copy(
            sc.d_send.at[level, side, me, units(piece)],
            new_w.at[level, units(piece), place],
            sc.own_out.at[level, side, piece],
        )

    def hand_back(level, side, piece):
        if side == 1:
            zcopy(1, level, piece).wait_recv()
        all_dcopies(level, side, piece).wait_send()

        def run(k, c):
            i = (me + 1 + k) % HALF
            named = table[level, pg.peer(i)]
            new = sc.fresh[level, named, units(piece), :] if side == 0 else far[level][piece][named]
            sc.d_send[level, side, i, units(piece), :] = new

            @pl.when(i != me)
            def _():
                ocopy(level, side, piece, i, me).start()

            @pl.when(i == me)
            def _():
                own_copy(level, side, piece).start()

            return c

        lax.fori_loop(0, HALF, run, 0)

    changes(1, 1, (0,))
    changes(1, 1, (1,))
    sums_across(1, 0)
    changes(0, 1, (1,))
    sums_across(1, 1)
    changes(0, 1, (0,))
    sums_across(0, 1)
    changes(1, 0, (0, 1))
    sums_across(0, 0)
    changes(0, 0, (0, 1))
    update(1, 0)
    update(1, 1)
    hand_back(1, 0, 0)
    hand_back(1, 0, 1)
    update(0, 1)
    update(0, 0)
    hand_back(1, 1, 0)
    hand_back(0, 0, 1)
    hand_back(0, 0, 0)
    hand_back(1, 1, 1)
    hand_back(0, 1, 1)
    hand_back(0, 1, 0)

    for level in (0, 1):
        for side in (0, 1):
            for piece in range(PIECES):
                own_copy(level, side, piece).wait()
                ref = sc.d_send.at[level, side, pl.ds(0, HALF - 1), units(piece)]
                others = pcopy(ref, ref, sc.os.at[level, side, piece], sc.orv.at[level, side, piece], pg.across)
                others.wait_recv()
                others.wait_send()
        for piece in range(PIECES):
            zcopy(0, level, piece).wait_send()
            zcopy(1, level, piece).wait_send()
            for c in outs(level, piece):
                c.wait()


def step_kernel(names, width_scale, hidden_scale, tokens, x_ref, t_ref, ids_ref, table_ref, w_ref, mast_ref, mom_ref,
                new_w_ref, new_mast_ref, new_mom_ref, *refs):
    sc = Refs(**dict(zip(names, refs)))
    pp = Place()
    pg = Group()
    x, z, w = pp.x, pp.z, pp.w
    own = [(c * OWN, rows_a(c, x, z), RA) for c in range(CHUNKS)] + [(c * OWN + RA, rows_b(c, x, z), RB) for c in range(CHUNKS)]

    mine = [
        pltpu.make_async_copy(x_ref.at[pl.ds(lo, n)], sc.xg.at[pl.ds(start, n)], sc.own.at[k // 2, k % 2])
        for k, (lo, start, n) in enumerate(own)
    ]
    loads = [
        pltpu.make_async_copy(w_ref.at[0], sc.w_in, sc.local.at[0]),
        pltpu.make_async_copy(w_ref.at[1], sc.w_out, sc.local.at[1]),
        pltpu.make_async_copy(t_ref, sc.tgt, sc.local.at[2]),
        pltpu.make_async_copy(mast_ref, sc.mast, sc.local.at[3]),
        pltpu.make_async_copy(mom_ref, sc.mom, sc.local.at[4]),
    ]
    for c in mine + loads:
        c.start()

    barrier = pltpu.get_barrier_semaphore()
    for f in (pp.right, pp.left, pp.inner):
        pl.semaphore_signal(barrier, inc=1, device_id={"fsdp": f}, device_id_type=MESH)

    @pl.when(w == 1)
    def _():
        pl.semaphore_signal(barrier, inc=1, device_id={"fsdp": pp.edge}, device_id_type=MESH)

    for i in range(HALF):

        @pl.when(pg.i != i)
        def _():
            pl.semaphore_signal(barrier, inc=1, device_id={"path": pg.peer(i)}, device_id_type=MESH)

    pl.semaphore_signal(barrier, inc=1, device_id={"path": pg.across}, device_id_type=MESH)
    pl.semaphore_wait(barrier, 3 + HALF + w)
    for c in mine + loads[:1]:
        c.wait()

    def across_width(rows, weights):
        return lax.dot_general(rows, weights[...], (((1,), (1,)), ((), ())), preferred_element_type=jnp.float32)

    def forward(start, n):
        rows = pl.ds(start, n)
        pre = across_width(sc.xg[rows, :], sc.w_in) * width_scale
        sig = jax.nn.sigmoid(pre)
        sc.act[rows, :] = (pre * sig).astype(jnp.bfloat16)
        sc.slope[rows, :] = sig * (1.0 + pre * (1.0 - sig))

    def partial(start, n, cs):
        return jnp.dot(sc.act[pl.ds(start, n), :], sc.w_out[:, cs], preferred_element_type=jnp.float32) * hidden_scale

    def loss_grad(total, lo, start, n):
        res = up(sc.xg[pl.ds(start, n), :]) + total - up(sc.tgt[pl.ds(lo, n), :])
        sc.og[pl.ds(start, n), :] = (sc.keep[pl.ds(lo, n), 0:1] * res / tokens).astype(jnp.bfloat16)

    def backward(start, n):
        rows = pl.ds(start, n)
        act_grad = across_width(sc.og[rows, :], sc.w_out) * hidden_scale
        sc.pre_grad[rows, :] = (act_grad * sc.slope[rows, :]).astype(jnp.bfloat16)

    first = [Gather(pp, c, sc.xg, sc.g_send, sc.g_recv, forward) for c in range(CHUNKS)]
    sums = [Reduce(pp, c, partial, sc) for c in range(CHUNKS)]
    second = [Gather(pp, c, sc.og, sc.g_send, sc.g_recv, backward) for c in range(CHUNKS)]

    def turn_over(c):
        sums[c].finish()
        loss_grad(sc.acc_a[c], *own[c])
        loss_grad(sc.fin_b[...], *own[CHUNKS + c])
        first[c].finish()
        second[c].start()

    def steps(*jobs):
        def run(k, carry):
            for job, offset in jobs:
                job.step(k + offset)
            return carry

        lax.fori_loop(0, STEPS // 2, run, 0)

    late = STEPS // 2
    first[0].start()
    steps((first[0], 0))
    first[1].start()
    steps((first[0], late), (first[1], 0))
    for c in loads[1:]:
        c.wait()
    kept = (ids_ref[...] >= SPECIAL).astype(jnp.float32)
    sc.keep[...] = jnp.broadcast_to(kept, sc.keep.shape).T
    steps((sums[0], 0), (first[1], late))
    steps((sums[0], late), (sums[1], 0))
    turn_over(0)
    steps((second[0], 0), (sums[1], late))
    turn_over(1)
    steps((second[0], late), (second[1], 0))
    steps((second[1], late))
    path_phase(pg, sc, width_scale, hidden_scale, table_ref, new_w_ref, new_mast_ref, new_mom_ref)
    for job in second:
        job.finish()
    for job in sums:
        job.drain()


def turn(v):
    return jnp.swapaxes(v, -1, -2)


def per_device(inputs, targets, token_ids, module_table, path_weights, master, momentum):
    width, hidden = path_weights.shape[2:]
    n = lax.axis_size("fsdp")
    tokens = inputs.shape[1] * n
    modules, rows = master.shape[1:3]
    spec = scratch(width, hidden, modules, rows)
    hbm = pl.BlockSpec(memory_space=pl.ANY)
    vmem = pl.BlockSpec(memory_space=pltpu.VMEM)
    smem = pl.BlockSpec(memory_space=pltpu.SMEM)
    new_weights, new_master, new_momentum = pl.pallas_call(
        functools.partial(step_kernel, tuple(spec), width ** (-0.5), (hidden * n) ** (-0.5), tokens),
        out_shape=(
            jax.ShapeDtypeStruct((2, hidden, width), jnp.bfloat16),
            jax.ShapeDtypeStruct((2, modules, hidden, rows), jnp.float32),
            jax.ShapeDtypeStruct((2, modules, hidden, rows), jnp.float32),
        ),
        in_specs=[hbm, hbm, vmem, smem, hbm, hbm, hbm],
        out_specs=(hbm, hbm, hbm),
        scratch_shapes=list(spec.values()),
        compiler_params=pltpu.CompilerParams(
            collective_id=0, has_side_effects=True, vmem_limit_bytes=63 * 1024 * 1024
        ),
        name="outer_step",
    )(inputs[0], targets[0], token_ids, module_table.T, turn(path_weights[0]), turn(master), turn(momentum))
    return (turn(new_weights)[None], turn(new_master), turn(new_momentum))


def solution(mesh):
    in_specs = (
        P("path", "fsdp", None),
        P("path", "fsdp", None),
        P("path", "fsdp"),
        P(),
        P("path", None, None, "fsdp"),
        P(None, None, "path", "fsdp"),
        P(None, None, "path", "fsdp"),
    )
    out_specs = (
        P("path", None, None, "fsdp"),
        P(None, None, "path", "fsdp"),
        P(None, None, "path", "fsdp"),
    )
    return jax.shard_map(
        per_device, mesh=mesh, in_specs=in_specs, out_specs=out_specs, check_vma=False
    )
```

time: 820 us -> 295 us (0.36)
  waiting for transfers between devices: 717 us -> 0 us
  Pallas kernels: 0 us -> 282 us
  matrix products: 42.1 us -> 0 us
  local copies, waits for them, and re-layouts: 29.3 us -> 6.86 us
  starting transfers between devices: 15.2 us -> 0 us
  between operations: 13.8 us -> 0.65 us
    all_gather x2 -> x0, waiting for transfers between devices: 374 us -> none  [the longest x1 188 us: per_device(): x_full = lax.all_gather(x_local, 'fsdp', axis=0, tiled=True)]
    pallas_call x0 -> x1, Pallas kernels: none -> 282 us  [per_device(): pl.pallas_call(functools.partial(step_kernel, tuple(spec), width ** (-0.5...]
    reduce_scatter x1 -> x0, waiting for transfers between devices: 185 us -> none  [per_device(): lax.psum_scatter((lax.dot_general(rows, w_out, (((1,), (1,)), ((), ())),...]
    all_to_all x2 -> x0, waiting for transfers between devices: 157 us -> none  [the longest x1 119 us: per_device(): lax.all_to_all(stacked.astype(jnp.bfloat16), 'path', split_axis=2, concat...]
    dot_general x6 -> x0, matrix products: 42.1 us -> none  [the longest x1 14.8 us: per_device(): lax.dot_general(x_full, pre_grad, (((0,), (0,)), ((), ())), preferred_ele...]
    all_to_all x2 -> x0, starting transfers between devices: 14.9 us -> none  [the longest x1 10.4 us: per_device(): lax.all_to_all(stacked.astype(jnp.bfloat16), 'path', split_axis=2, concat...]
    all_to_all x2 -> x0, local copies, waits for them, and re-layouts: 8.56 us -> none  [the longest x1 5.13 us: per_device(): lax.all_to_all(stacked.astype(jnp.bfloat16), 'path', split_axis=2, concat...]
  transfers between devices with their start and end apart: 5 -> 0, of which waited for: 5 -> 0; matrix products, arithmetic and copies ran while one was open for 0% -> 0% of each run, Pallas kernels for 0% -> 0%
where the time goes in v3:
time: 295 us; the launch traced here: 290 us
  Pallas kernels  282 us (96%)
  local copies, waits for them, and re-layouts  6.86 us (2%)
    pallas_call x1, Pallas kernels, per_device(): pl.pallas_call(functools.partial(step_kernel, tuple(spec), width ** (-0.5...  282 us
    unnamed x7, local copies, waits for them, and re-layouts  6.86 us

profile of v3, /device:TPU:121, one launch (start us, length us, event | category | flops | bytes accessed | tf_op | source)
XLA Modules:
  0.0 290.0 jit_solution(15537220500015252661)
XLA Ops:
  0.6 282.5 %outer_step.1 = (bf16[2,352,2048]{2,1,0:T(8,128)(2,1)}, f32[2,4,352,128]{3,2,1,0:T(8,128)}, f32[2,4,352,128]{3,2,1,0:T(8,128)}) custom-call(bf16[128,2048]{1,0:T(8,128)(2,1)} %bitcast.19, bf16[128,2048]{1,0:T(8,128)(2,1)} %bitcast.20, s32[1,128]{1,0:T(1,128)} %ids_ref.1, s32[2,16]{1,0:T(2,128)} %bitcast.21, bf16[2,352,2048]{2,1,0:T(8,128)(2,1)} %bitcast.13, ...), custom_call_target="tpu_custom_call" | custom-call | tf_op jit(solution)/shard_map/outer_step/pallas_call | solution.py:776
  283.1 0.0 copy-start.1
  283.1 3.9 %copy.13 = bf16[1,2,2048,352]{2,3,1,0:T(8,128)(2,1)} copy(bf16[1,2,2048,352]{2,3,1,0:T(8,128)(2,1)} %bitcast.14) | data formatting | bytes 5767168
  287.0 0.0 copy-done.1
  287.0 0.0 copy-start
  287.0 1.1 copy.14
  288.1 0.8 copy-done
  288.9 1.1 copy.15
Async XLA Ops:
  283.1 3.9 %copy-start.1 = (f32[2,4,352,128]{3,2,1,0:T(8,128)S(1)}, f32[2,4,352,128]{3,2,1,0:T(8,128)}, u32[]{:S(2)}) copy-start(f32[2,4,352,128]{3,2,1,0:T(8,128)} %get-tuple-element.7) | copy-start | bytes 4325380
  287.0 1.9 copy-start

commit v4 on v3

--- a/solution.py
+++ b/solution.py
@@ -166,16 +166,22 @@
             self.arrived(5, 0, zl, ref)
             self.z_forward(5, t - 1, zl, ref)
 
-        @pl.when((t >= 1) & (t <= 4))
-        def _():
-            self.compute(rows_super(c, zl), SUPER)
-
         @pl.when(t >= 2)
         def _():
             zo = pp.zb(t - 2)
             for side in (0, 1):
                 self.arrived(2, side, t - 2, self.piece(rows_a(c, pp.col(2), zo), RA, side))
-            self.compute(rows_line(c, zo), LINE)
+
+    def work(self, t):
+        pp, c = self.pp, self.chunk
+
+        @pl.when((t >= 1) & (t <= 4))
+        def _():
+            self.compute(rows_super(c, pp.zb(t - 1)), SUPER)
+
+        @pl.when(t >= 2)
+        def _():
+            self.compute(rows_line(c, pp.zb(t - 2)), LINE)
 
     def finish(self):
         for kind, n in ((0, RA), (5, SUPER)):
@@ -285,6 +291,23 @@
         self.over(fill)
         self.z_stage(4, r, sc.acc_b, sc.b_recv, sc.b_send)
 
+    def fill(self, r):
+        sc, c = self.sc, self.chunk
+        start = rows_line(c, self.pp.zb(r))
+
+        def body(cs):
+            sc.part[c, r, :, cs] = self.partial(start, LINE, cs).astype(jnp.bfloat16)
+
+        self.over(body)
+
+    def start(self):
+        self.fill(3)
+
+    def work(self, t):
+        @pl.when(t <= 2)
+        def _():
+            self.fill(2 - t)
+
     def step(self, t):
         pp, sc, c, w = self.pp, self.sc, self.chunk, self.pp.w
         r0, r1, r2 = 3 - t, 4 - t, 5 - t
@@ -297,12 +320,6 @@
 
         @pl.when(t <= 3)
         def _():
-            start = rows_line(c, pp.zb(r0))
-
-            def fill(cs):
-                sc.part[c, r0, :, cs] = self.partial(start, LINE, cs).astype(jnp.bfloat16)
-
-            self.over(fill)
             for side, _, f, lo in sides:
                 src = sc.part.at[c, r0, rows(2, RA), pl.ds(lo, half)]
                 self.push(src, sc.h_recv.at[c, side, r0], 0, side, r0, f, (side, r0))
@@ -733,6 +750,8 @@
         def run(k, carry):
             for job, offset in jobs:
                 job.step(k + offset)
+            for job, offset in jobs:
+                job.work(k + offset)
             return carry
 
         lax.fori_loop(0, STEPS // 2, run, 0)
@@ -746,7 +765,9 @@
         c.wait()
     kept = (ids_ref[...] >= SPECIAL).astype(jnp.float32)
     sc.keep[...] = jnp.broadcast_to(kept, sc.keep.shape).T
+    sums[0].start()
     steps((sums[0], 0), (first[1], late))
+    sums[1].start()
     steps((sums[0], late), (sums[1], 0))
     turn_over(0)
     steps((second[0], 0), (sums[1], late))
@@ -758,6 +779,43 @@
         job.finish()
     for job in sums:
         job.drain()
+
+
+LANES = 4
+
+
+def land_kernel(*refs):
+    count = (len(refs) - 2) // 3
+    sems_in, sems_out = refs[-2:]
+    ins, outs = [], []
+    for k in range(count):
+        src, dst, stage = refs[k], refs[count + k], refs[2 * count + k]
+        size = src.shape[-2] // LANES // 16 * 16
+        for lane in range(LANES):
+            n = size if lane < LANES - 1 else src.shape[-2] - lane * size
+            where = (slice(None),) * (len(src.shape) - 2) + (pl.ds(lane * size, n),)
+            ins.append(pltpu.make_async_copy(src.at[where], stage.at[where], sems_in.at[k, lane]))
+            outs.append(pltpu.make_async_copy(stage.at[where], dst.at[where], sems_out.at[k, lane]))
+    for c in ins:
+        c.start()
+    for got, put in zip(ins, outs):
+        got.wait()
+        put.start()
+    for c in outs:
+        c.wait()
+
+
+def land(*arrays):
+    hbm = pl.BlockSpec(memory_space=pl.ANY)
+    return pl.pallas_call(
+        land_kernel,
+        out_shape=tuple(jax.ShapeDtypeStruct(v.shape, v.dtype) for v in arrays),
+        in_specs=[hbm] * len(arrays),
+        out_specs=(hbm,) * len(arrays),
+        scratch_shapes=[pltpu.VMEM(v.shape, v.dtype) for v in arrays] + [pltpu.SemaphoreType.DMA((len(arrays), LANES))] * 2,
+        compiler_params=pltpu.CompilerParams(vmem_limit_bytes=60 * 1024 * 1024),
+        name="land",
+    )(*arrays)
 
 
 def turn(v):
@@ -788,6 +846,7 @@
         ),
         name="outer_step",
     )(inputs[0], targets[0], token_ids, module_table.T, turn(path_weights[0]), turn(master), turn(momentum))
+    new_weights, new_master, new_momentum = land(new_weights, new_master, new_momentum)
     return (turn(new_weights)[None], turn(new_master), turn(new_momentum))
 
 

time: 295 us -> 290 us (0.983)
  local copies, waits for them, and re-layouts: 6.86 us -> 0 us
  Pallas kernels: 282 us -> 285 us
    unnamed x7 -> x0, local copies, waits for them, and re-layouts: 6.86 us -> none
    pallas_call x0 -> x1, Pallas kernels: none -> 5.16 us  [land(): pl.pallas_call(land_kernel, out_shape=tuple((jax.ShapeDtypeStruct(v.shape...]
    pallas_call x1, Pallas kernels: 282 us -> 279 us  [per_device(): pl.pallas_call(functools.partial(step_kernel, tuple(spec), width ** (-0.5...]
where the time goes in v4:
time: 290 us; the launch traced here: 285 us
  Pallas kernels  285 us (98%)
    pallas_call x1, Pallas kernels, per_device(): pl.pallas_call(functools.partial(step_kernel, tuple(spec), width ** (-0.5...  279 us

profile of v4, /device:TPU:121, one launch (start us, length us, event | category | flops | bytes accessed | tf_op | source)
XLA Modules:
  0.0 285.3 jit_solution(3166489428139002879)
XLA Ops:
  0.6 279.4 %outer_step.1 = (bf16[2,352,2048]{2,1,0:T(8,128)(2,1)}, f32[2,4,352,128]{3,2,1,0:T(8,128)}, f32[2,4,352,128]{3,2,1,0:T(8,128)}) custom-call(bf16[128,2048]{1,0:T(8,128)(2,1)} %bitcast.16, bf16[128,2048]{1,0:T(8,128)(2,1)} %bitcast.17, s32[1,128]{1,0:T(1,128)} %ids_ref.1, s32[2,16]{1,0:T(2,128)} %bitcast.18, bf16[2,352,2048]{2,1,0:T(8,128)(2,1)} %bitcast.13, ...), custom_call_target="tpu_custom_call" | custom-call | tf_op jit(solution)/shard_map/outer_step/pallas_call | solution.py:834
  280.0 5.2 %land.1 = (bf16[2,352,2048]{2,1,0:T(8,128)(2,1)}, f32[2,4,352,128]{3,2,1,0:T(8,128)}, f32[2,4,352,128]{3,2,1,0:T(8,128)}) custom-call(bf16[2,352,2048]{2,1,0:T(8,128)(2,1)} %get-tuple-element.9.refs_0_, f32[2,4,352,128]{3,2,1,0:T(8,128)} %get-tuple-element.10.refs_1_, f32[2,4,352,128]{3,2,1,0:T(8,128)} %get-tuple-element.11.refs_2_), custom_call_target="tpu_custom_call" | custom-call | tf_op jit(solution)/shard_map/land/pallas_call | solution.py:810

commit v5 on v4

--- a/solution.py
+++ b/solution.py
@@ -589,7 +589,8 @@
             sc.fresh[level, m, part, :] = master.astype(jnp.bfloat16)
 
         sums(level, 0, piece, use)
-        zcopy(1, level, piece).start()
+        if (level, piece) != (0, 0):
+            zcopy(1, level, piece).start()
         for c in outs(level, piece):
             c.start()
 
@@ -637,15 +638,15 @@
     changes(1, 1, (0,))
     changes(1, 1, (1,))
     sums_across(1, 0)
+    changes(1, 0, (0, 1))
+    sums_across(1, 1)
     changes(0, 1, (1,))
-    sums_across(1, 1)
     changes(0, 1, (0,))
+    update(1, 0)
     sums_across(0, 1)
-    changes(1, 0, (0, 1))
     sums_across(0, 0)
+    update(1, 1)
     changes(0, 0, (0, 1))
-    update(1, 0)
-    update(1, 1)
     hand_back(1, 0, 0)
     hand_back(1, 0, 1)
     update(0, 1)
@@ -654,6 +655,8 @@
     hand_back(0, 0, 1)
     hand_back(0, 0, 0)
     hand_back(1, 1, 1)
+    zcopy(1, 0, 1).wait_send()
+    zcopy(1, 0, 0).start()
     hand_back(0, 1, 1)
     hand_back(0, 1, 0)
 
@@ -667,7 +670,8 @@
                 others.wait_send()
         for piece in range(PIECES):
             zcopy(0, level, piece).wait_send()
-            zcopy(1, level, piece).wait_send()
+            if (level, piece) != (0, 1):
+                zcopy(1, level, piece).wait_send()
             for c in outs(level, piece):
                 c.wait()
 

time: 290 us -> 290 us (level)
  the two profiles are of different devices: /device:TPU:121 before, /device:TPU:35 now
where the time goes in v5:
time: 290 us
  Pallas kernels  289 us (100%)
    pallas_call x1, Pallas kernels, per_device(): pl.pallas_call(functools.partial(step_kernel, tuple(spec), width ** (-0.5...  284 us

profile of v5, /device:TPU:35, one launch (start us, length us, event | category | flops | bytes accessed | tf_op | source)
XLA Modules:
  0.0 290.1 jit_solution(15319778486654832611)
XLA Ops:
  0.6 284.2 %outer_step.1 = (bf16[2,352,2048]{2,1,0:T(8,128)(2,1)}, f32[2,4,352,128]{3,2,1,0:T(8,128)}, f32[2,4,352,128]{3,2,1,0:T(8,128)}) custom-call(bf16[128,2048]{1,0:T(8,128)(2,1)} %bitcast.16, bf16[128,2048]{1,0:T(8,128)(2,1)} %bitcast.17, s32[1,128]{1,0:T(1,128)} %ids_ref.1, s32[2,16]{1,0:T(2,128)} %bitcast.18, bf16[2,352,2048]{2,1,0:T(8,128)(2,1)} %bitcast.13, ...), custom_call_target="tpu_custom_call" | custom-call | tf_op jit(solution)/shard_map/outer_step/pallas_call | solution.py:838
  284.8 5.2 %land.1 = (bf16[2,352,2048]{2,1,0:T(8,128)(2,1)}, f32[2,4,352,128]{3,2,1,0:T(8,128)}, f32[2,4,352,128]{3,2,1,0:T(8,128)}) custom-call(bf16[2,352,2048]{2,1,0:T(8,128)(2,1)} %get-tuple-element.9.refs_0_, f32[2,4,352,128]{3,2,1,0:T(8,128)} %get-tuple-element.10.refs_1_, f32[2,4,352,128]{3,2,1,0:T(8,128)} %get-tuple-element.11.refs_2_), custom_call_target="tpu_custom_call" | custom-call | tf_op jit(solution)/shard_map/land/pallas_call | solution.py:814
